TPU v7x, 32 devices: a whole 2x2x4 slice. The times are simulated.
32 devices in a mesh: group: 2 (over y), expert: 4 (over z), dp: 4 (over x, core).
Axes of the slice: x: 2, y: 2, z: 4, core: 2. Of those that a mesh axis runs over, the one named last changes fastest.
Arguments:
- tokens: bfloat16 [1536, 6144], P(('group', 'expert'), 'dp'), parts along dimension 0, may hold values from -6 to 6
- out_grad: bfloat16 [1536, 6144], P(('group', 'expert'), 'dp'), parts along dimension 0, may hold values from -0.59765625 to 0.59765625
- gate_probs: float32 [1536, 4], P(('group', 'expert')), parts along dimension 0, may hold values from 0.1 to 1
- routes: int32 [1536, 4], P(('group', 'expert')), parts along dimension 0, may hold values from 0 to 15, as said below
- expert_weights: bfloat16 [3, 10752, 6144], P(None, 'expert', 'dp'), may hold values from -0.078125 to 0.078125
Outputs:
- weight_grads: float32 [6, 10752, 6144], P('group', 'expert', 'dp'), parts along dimension 0
There are 2 independent parts, one for each index of `group`. A program takes and returns all parts, laid end to end along the dimension named above; an argument that names none is the same for every part. Nothing has to cross between parts.
Inputs may be any that keep to these rules, and one draw needn't show every extreme that they name: `routes`: each row names 4 different experts. Among the 192 rows held by one device along `expert`, expert 0 is named by at most 48 rows, and in every draw some device along `expert` has exactly 48 such rows.
All inputs are finite; a program needn't handle non-finite values.
Results may differ from a plain program's by a relative error of at most 0.0041.
Values may be sent and summed in bfloat16 or wider, within the bound.
No kernel may reach another device: no remote copies, remote signals or barrier semaphores. Data moves between devices by JAX's collectives and lax.ppermute only.
A program may use at most 256 MiB of HBM per device.

v0:
```python
import jax
import jax.numpy as jnp
from jax import lax
from jax.sharding import PartitionSpec as P


def activations(gate_up, down_grad, width):
    gate = gate_up[:, :width]
    up = gate_up[:, width:]
    sig = jax.nn.sigmoid(gate)
    hidden = (gate * sig * up).astype(jnp.bfloat16)
    gate_grad = down_grad * up * sig * (1.0 + gate * (1.0 - sig))
    up_grad = down_grad * gate * sig
    left = jnp.concatenate([gate_grad, up_grad], axis=1).astype(jnp.bfloat16)
    return (left, hidden)


def contract_last(left, right):
    return lax.dot_general(
        left, right, (((1,), (1,)), ((), ())), preferred_element_type=jnp.float32
    )


def contract_first(left, right):
    return lax.dot_general(
        left, right, (((0,), (0,)), ((), ())), preferred_element_type=jnp.float32
    )


def per_device(tokens, out_grad, gate_probs, routes, expert_weights):
    tok_rows, slice_width = tokens.shape
    hid_local = expert_weights.shape[1]
    capacity = tok_rows // 4
    hit = routes == 0
    token_hit = jnp.any(hit, axis=1)
    prob = jnp.sum(jnp.where(hit, gate_probs, jnp.zeros_like(gate_probs)), axis=1)
    flags = token_hit.astype(jnp.int32)
    before = jnp.cumsum(flags, dtype=jnp.int32) - flags
    match = token_hit[None, :] & (before[None, :] == jnp.arange(capacity, dtype=jnp.int32)[:, None])
    picker = match.astype(jnp.bfloat16)
    scaled = (out_grad.astype(jnp.float32) * prob[:, None]).astype(jnp.bfloat16)
    rows_x = jnp.dot(picker, tokens, preferred_element_type=jnp.float32).astype(jnp.bfloat16)
    rows_dy = jnp.dot(picker, scaled, preferred_element_type=jnp.float32).astype(jnp.bfloat16)
    stacked = jnp.stack([rows_x, rows_dy])
    moved = lax.all_gather(stacked, "expert", axis=1, tiled=True)
    w_gateup = expert_weights[:2].reshape(2 * hid_local, slice_width)
    partial_value = jnp.concatenate(
        [contract_last(moved[0], w_gateup), contract_last(moved[1], expert_weights[2])], axis=1
    )
    summed = lax.psum(partial_value, "dp")
    left, hidden = activations(summed[:, : 2 * hid_local], summed[:, 2 * hid_local :], hid_local)
    part_gu = contract_first(left, moved[0])
    part_down = contract_first(hidden, moved[1])
    return jnp.concatenate([part_gu, part_down], axis=0).reshape(3, hid_local, slice_width)


def solution(mesh):
    in_specs = (
        P(("group", "expert"), "dp"),
        P(("group", "expert"), "dp"),
        P(("group", "expert"), None),
        P(("group", "expert"), None),
        P(None, "expert", "dp"),
    )
    out_specs = P("group", "expert", "dp")
    return jax.shard_map(
        per_device, mesh=mesh, in_specs=in_specs, out_specs=out_specs, check_vma=False
    )
```

profile of v0, /device:TPU:21, one launch (start us, length us, event | category | flops | bytes accessed | tf_op | source)
XLA Modules:
  0.0 252.2 jit_solution(2032044244761758988)
XLA Ops:
  6.5 0.0 copy-start
  6.5 0.0 all-gather.2.cloned.1.call-start
  6.5 0.8 fusion.22
  7.3 0.3 reduce-window.9
  7.6 0.1 slice.36
  7.8 0.1 slice_reduce_fusion
  7.9 0.1 add_bitcast_fusion
  8.0 0.7 select_reduce_fusion
  8.7 0.0 copy-done
  8.7 0.2 fusion.3
  8.9 1.4 fusion.4
  10.3 0.7 pad_maximum_fusion.2
  11.0 0.0 all-gather.2.cloned.1.call-update
  11.0 0.0 all-reduce.3.cloned.1.call-start
  11.1 13.7 %slice.40 = bf16[2,2688,1536]{2,1,0:T(8,128)(2,1)} slice(bf16[3,2688,1536]{2,1,0:T(8,128)(2,1)} %param.9), slice={[0:2], [0:2688], [0:1536]} | slice | bytes 33030144 | tf_op jit(solution)/shard_map/slice | solution.py:46
  24.8 17.0 %all-gather.2.cloned.1.call-done = bf16[2,192,1536]{2,1,0:T(8,128)(2,1)} async-done(((bf16[2,48,1536]{2,1,0:T(8,128)(2,1)}), bf16[2,192,1536]{2,1,0:T(8,128)(2,1)}) %all-gather.2.cloned.1.call-update) | async-done | bytes 1179664 | tf_op jit(solution)/shard_map/all_gather | solution.py:45
  41.8 6.4 %fusion = f32[192,2688]{1,0:T(8,128)S(1)} fusion(bf16[3,2688,1536]{2,1,0:T(8,128)(2,1)} %param.9, bf16[2,192,1536]{2,1,0:T(8,128)(2,1)} %all-gather.2.cloned.1.call-done), kind=kOutput, calls=%fused_computation.1 | convolution fusion | flops 1585446912 | bytes 10911744 | tf_op jit(solution)/shard_map/dot_general | solution.py:19
  48.1 13.2 %fusion.12 = f32[192,5376]{1,0:T(8,128)} fusion(bf16[5376,1536]{1,0:T(8,128)(2,1)} %bitcast.23, bf16[2,192,1536]{2,1,0:T(8,128)(2,1)} %all-gather.2.cloned.1.call-done), kind=kOutput, calls=%fused_computation.23 | convolution fusion | flops 3170893824 | bytes 21233664 | tf_op jit(solution)/shard_map/dot_general | solution.py:19
  61.4 5.2 %pad_maximum_fusion.1 = f32[192,8064]{1,0:T(8,128)} fusion(f32[192,2688]{1,0:T(8,128)S(1)} %fusion, f32[192,5376]{1,0:T(8,128)} %fusion.12), kind=kLoop, calls=%fused_computation.4 | loop fusion | flops 1548288 | bytes 12386304 | tf_op jit(solution)/shard_map/concatenate | solution.py:47
  66.6 0.0 all-reduce.3.cloned.1.call-update
  66.6 0.0 copy-start.2
  66.6 117.9 %all-reduce.3.cloned.1.call-done = f32[192,8064]{1,0:T(8,128)} async-done(((f32[192,8064]{1,0:T(8,128)}), f32[192,8064]{1,0:T(8,128)}) %all-reduce.3.cloned.1.call-update) | async-done | bytes 6193168 | tf_op jit(solution)/shard_map/psum | solution.py:50
  184.5 3.8 %multiply_convert_fusion.2 = (bf16[192,2688]{1,0:T(8,128)(2,1)S(1)}, bf16[192,2688]{1,0:T(8,128)(2,1)S(1)}) fusion(f32[192,8064]{1,0:T(8,128)} %all-reduce.3.cloned.1.call-done), kind=kLoop, calls=%fused_computation.15 | loop fusion | flops 6709248 | bytes 8257536 | tf_op jit(solution)/shard_map/convert
  188.3 0.0 copy-done.2
  188.3 10.3 %fusion.9 = f32[2688,1536]{1,0:T(8,128)} fusion(f32[192,8064]{1,0:T(8,128)} %all-reduce.3.cloned.1.call-done, bf16[2,192,1536]{2,1,0:T(8,128)(2,1)S(1)} %copy-done.2), kind=kOutput, calls=%fused_computation.18 | convolution fusion | flops 1588543488 | bytes 21233664 | tf_op jit(solution)/shard_map/dot_general | solution.py:25
  198.6 13.0 %fusion.5 = f32[5376,1536]{1,0:T(8,128)} fusion(bf16[192,2688]{1,0:T(8,128)(2,1)S(1)} %get-tuple-element.8, bf16[192,2688]{1,0:T(8,128)(2,1)S(1)} %get-tuple-element.7, bf16[2,192,1536]{2,1,0:T(8,128)(2,1)S(1)} %copy-done.2), kind=kOutput, calls=%fused_computation.9 | convolution fusion | flops 3175022592 | bytes 35684352 | tf_op jit(solution)/shard_map/dot_general | solution.py:25
  211.6 0.0 copy-start.1
  211.6 33.8 %pad_maximum_fusion = f32[8064,1536]{1,0:T(8,128)} fusion(f32[2688,1536]{1,0:T(8,128)} %fusion.9, f32[5376,1536]{1,0:T(8,128)} %fusion.5), kind=kLoop, calls=%fused_computation | loop fusion | flops 12386304 | bytes 99090432 | tf_op jit(solution)/shard_map/concatenate | solution.py:54
  245.4 0.0 copy-done.1
  (4 shorter events, 0.1 us)
Async XLA Ops:
  6.5 2.1 copy-start
  6.5 35.2 %all-gather.2.cloned.1.call-start = ((), (), s32[]{:S(2)}) async-start(), calls=%async_computation | async-start | bytes 1474560 | tf_op jit(solution)/shard_map/all_gather | solution.py:45
  11.0 173.5 %all-reduce.3.cloned.1.call-start = ((), (), s32[]{:S(2)}) async-start(), calls=%async_computation.1 | async-start | bytes 12386304 | tf_op jit(solution)/shard_map/psum | solution.py:50
  66.6 121.7 %copy-start.2 = (bf16[2,192,1536]{2,1,0:T(8,128)(2,1)S(1)}, bf16[2,192,1536]{2,1,0:T(8,128)(2,1)}, u32[]{:S(2)}) copy-start(bf16[2,192,1536]{2,1,0:T(8,128)(2,1)} %all-gather.2.cloned.1.call-done) | copy-start | bytes 3538948
  211.6 33.8 %copy-start.1 = (bf16[192,1536]{1,0:T(8,128)(2,1)S(1)}, bf16[192,1536]{1,0:T(8,128)(2,1)}, u32[]{:S(2)}) copy-start(bf16[192,1536]{1,0:T(8,128)(2,1)} %param.5) | copy-start | bytes 1769476
Sparse Core Ops, SparseCore 0:
  11.1 30.5 all-gather.1
  66.8 117.7 all-reduce.2
where the time goes:
time: 254 us; the launch traced here: 252 us
  waiting for transfers between devices  135 us (53%)
  other arithmetic  45.4 us (18%)
  matrix products  44.5 us (18%)
  local copies, waits for them, and re-layouts  13.9 us (5%)
  between operations  13.5 us (5%)
    psum x1, waiting for transfers between devices, per_device(): summed = lax.psum(partial_value, 'dp')  118 us
    concatenate x1, other arithmetic, per_device(): jnp.concatenate([part_gu, part_down], axis=0)  33.8 us
    dot_general x2, matrix products, contract_first(): lax.dot_general(left, right, (((0,), (0,)), ((), ())), preferred_element_...  23.3 us
    dot_general x2, matrix products, contract_last(): lax.dot_general(left, right, (((1,), (1,)), ((), ())), preferred_element_...  19.6 us
    all_gather x1, waiting for transfers between devices, per_device(): moved = lax.all_gather(stacked, 'expert', axis=1, tiled=True)  17 us
    slice x1, local copies, waits for them, and re-layouts, per_device(): w_gateup = expert_weights[:2].reshape(2 * hid_local, slice_width)  13.7 us
    concatenate x1, other arithmetic, per_device(): jnp.concatenate([contract_last(moved[0], w_gateup), contract_last(moved[1...  5.24 us
  transfers between devices with their start and end apart: 2, of which 2 were waited for; matrix products, arithmetic and copies ran while one was open for 5% of the time, Pallas kernels for 0%

commit v1 on v0

v1 whole, which is shorter than its diff:
```python
import functools

import jax
import jax.numpy as jnp
from jax import lax
from jax.experimental import pallas as pl
from jax.experimental.pallas import tpu as pltpu
from jax.sharding import PartitionSpec as P

STEP = 384
REST_CHUNKS = (2, 2, 2, 1)
VMEM = 24 * 1024 * 1024
SMALL = 8 * 1024 * 1024
FLOPS = 10**10


def contract_last(left, right):
    return lax.dot_general(
        left, right, (((1,), (1,)), ((), ())), preferred_element_type=jnp.float32
    )


def contract_first(left, right):
    return lax.dot_general(
        left, right, (((0,), (0,)), ((), ())), preferred_element_type=jnp.float32
    )


def activations(gate, up, down_grad):
    sig = jax.nn.sigmoid(gate)
    hidden = gate * sig * up
    gate_grad = down_grad * up * sig * (1.0 + gate * (1.0 - sig))
    up_grad = down_grad * gate * sig
    return jnp.stack([gate_grad, up_grad, hidden]).astype(jnp.bfloat16)


def pick_rows(tokens, out_grad, gate_probs, routes, flip):
    capacity = tokens.shape[0] // 4
    hit = routes == 0
    token_hit = jnp.any(hit, axis=1)
    prob = jnp.sum(jnp.where(hit, gate_probs, jnp.zeros_like(gate_probs)), axis=1)
    flags = token_hit.astype(jnp.int32)
    before = jnp.cumsum(flags, dtype=jnp.int32) - flags
    place = jnp.arange(capacity, dtype=jnp.int32)
    place = jnp.where(flip, lax.rem(place + capacity // 2, capacity), place)
    match = token_hit[None, :] & (before[None, :] == place[:, None])
    picker = match.astype(jnp.bfloat16)
    scaled = (out_grad.astype(jnp.float32) * prob[:, None]).astype(jnp.bfloat16)
    rows_x = jnp.dot(picker, tokens, preferred_element_type=jnp.float32).astype(jnp.bfloat16)
    rows_dy = jnp.dot(picker, scaled, preferred_element_type=jnp.float32).astype(jnp.bfloat16)
    return jnp.stack([rows_x, rows_dy])


def call(kernel, name, args, in_specs, out_specs, out_shape, after=(), grid=(), aliases=None, vmem=SMALL, flops=1000):
    return pl.pallas_call(
        kernel,
        grid=grid,
        in_specs=list(in_specs) + [pl.BlockSpec(memory_space=pl.ANY)] * len(after),
        out_specs=out_specs,
        out_shape=out_shape,
        input_output_aliases=aliases or {},
        compiler_params=pltpu.CompilerParams(vmem_limit_bytes=vmem),
        cost_estimate=pl.CostEstimate(flops=flops, bytes_accessed=1000, transcendentals=0),
        name=name,
    )(*args, *after)


def own_kernel(rows_ref, w_ref, own_ref, send_ref, kept_ref, sems):
    half = own_ref.shape[1]
    steps = kept_ref.shape[1] // STEP

    def piece(i):
        here = pl.ds(pl.multiple_of(i * STEP, STEP), STEP)
        return pltpu.make_async_copy(w_ref.at[:, here, :], kept_ref.at[:, here, :], sems.at[i])

    for i in range(steps):
        piece(i).start()

    def step(i, carry):
        piece(i).wait()
        here = pl.ds(pl.multiple_of(i * STEP, STEP), STEP)
        w = kept_ref[:, here, :]
        gate_up = contract_last(rows_ref[0], w[:2].reshape(2 * STEP, w.shape[2]))
        down = contract_last(rows_ref[1], w[2])
        for m, part in enumerate((gate_up[:, :STEP], gate_up[:, STEP:], down)):
            own_ref[m, :, here] = part[:half]
            send_ref[m, :, here] = part[half:].astype(jnp.bfloat16)
        return carry

    lax.fori_loop(0, steps, step, 0)


def forward_own(rows, weights):
    half, hid = rows.shape[1] // 2, weights.shape[1]
    return pl.pallas_call(
        own_kernel,
        in_specs=[pl.BlockSpec(memory_space=pltpu.VMEM), pl.BlockSpec(memory_space=pl.ANY)],
        out_specs=[pl.BlockSpec(memory_space=pltpu.VMEM)] * 3,
        out_shape=[
            jax.ShapeDtypeStruct((3, half, hid), jnp.float32),
            jax.ShapeDtypeStruct((3, half, hid), jnp.bfloat16),
            pltpu.VMEM(weights.shape, weights.dtype),
        ],
        scratch_shapes=[pltpu.SemaphoreType.DMA((hid // STEP,))],
        compiler_params=pltpu.CompilerParams(vmem_limit_bytes=SMALL),
        cost_estimate=pl.CostEstimate(flops=1000, bytes_accessed=1000, transcendentals=0),
        name="forward_own",
    )(rows, weights)


def forward_kernel(first, top, rows_ref, w_ref, *refs):
    own_ref, send_ref = refs[-2:]
    half, step = own_ref.shape[1:]
    start = pl.multiple_of((first + pl.program_id(0)) * step, step)
    w = w_ref[:, pl.ds(start, step), :]
    gate_up = contract_last(rows_ref[0, top:, :], w[:2].reshape(2 * step, w.shape[2]))
    down = contract_last(rows_ref[1, top:, :], w[2])
    for m, part in enumerate((gate_up[:, :step], gate_up[:, step:], down)):
        own_ref[m] = part[:half]
        send_ref[m] = part[half:].astype(jnp.bfloat16)


def forward(rows, top, weights, first, steps, after):
    _, count, width = rows.shape
    half, chunk = (count - top) // 2, steps * STEP
    return call(
        functools.partial(forward_kernel, first, top),
        "forward",
        (rows, weights),
        [
            pl.BlockSpec((2, count, width), lambda i: (0, 0, 0)),
            pl.BlockSpec(memory_space=pltpu.VMEM),
        ],
        [pl.BlockSpec((3, half, STEP), lambda i: (0, 0, i))] * 2,
        [
            jax.ShapeDtypeStruct((3, half, chunk), jnp.float32),
            jax.ShapeDtypeStruct((3, half, chunk), jnp.bfloat16),
        ],
        after,
        (steps,),
        flops=FLOPS,
    )


def backward_kernel(a_ref, b_ref, c_ref, d_ref, rows_ref, *refs):
    out_ref = refs[-1]
    for m in range(3):
        parts = [ref[m].astype(jnp.float32) for ref in (a_ref, b_ref, c_ref, d_ref)]
        left = jnp.concatenate(parts, axis=0).astype(jnp.bfloat16)
        out_ref[m] = contract_first(left, rows_ref[m // 2])


def backward(lefts, rows, grads, shape, first, steps, after):
    _, count, width = rows.shape
    in_specs = [
        pl.BlockSpec(
            (3, v.shape[1], STEP), lambda i, k=first if v.shape[2] == shape[1] else 0: (0, 0, k + i)
        )
        for v in lefts
    ] + [pl.BlockSpec((2, count, width), lambda i: (0, 0, 0))]
    args, aliases = list(lefts) + [rows], {}
    if grads is not None:
        after, aliases = (grads,) + after, {len(args): 0}
    return call(
        backward_kernel,
        "backward",
        args,
        in_specs,
        pl.BlockSpec((3, STEP, width), lambda i: (0, first + i, 0)),
        jax.ShapeDtypeStruct(shape, jnp.float32),
        after,
        (steps,),
        aliases,
        VMEM,
    )


def add_kernel(own_ref, received_ref, *refs):
    total = own_ref[...] + received_ref[...].astype(jnp.float32)
    refs[-2][...] = total
    refs[-1][...] = total.astype(jnp.bfloat16)


def act_kernel(pieces, *refs):
    left_ref, start = refs[-1], 0
    for k in range(pieces):
        total_ref, received_ref = refs[2 * k : 2 * k + 2]
        here = slice(start, start + total_ref.shape[2])
        start += total_ref.shape[2]
        gate, up, down_grad = [total_ref[m] + received_ref[m].astype(jnp.float32) for m in range(3)]
        sig = jax.nn.sigmoid(gate)
        left_ref[0, :, here] = (down_grad * up * sig * (1.0 + gate * (1.0 - sig))).astype(jnp.bfloat16)
        left_ref[1, :, here] = (down_grad * gate * sig).astype(jnp.bfloat16)
        left_ref[2, :, here] = (gate * sig * up).astype(jnp.bfloat16)


def add(own, received, after):
    whole = [pl.BlockSpec(memory_space=pltpu.VMEM)] * 2
    shapes = [jax.ShapeDtypeStruct(own.shape, t) for t in (jnp.float32, jnp.bfloat16)]
    return call(add_kernel, "add", (own, received), whole, whole, shapes, after)


def activate(sums, after):
    whole = pl.BlockSpec(memory_space=pltpu.VMEM)
    args = [v for pair in sums for v in pair]
    three, half, _ = args[0].shape
    shape = jax.ShapeDtypeStruct((three, half, sum(v.shape[2] for v, _ in sums)), jnp.bfloat16)
    kernel = functools.partial(act_kernel, len(sums))
    return call(kernel, "activate", args, [whole] * len(args), whole, shape, after)


def arrange_kernel(own_ref, lower_ref, upper_ref, far_lower_ref, far_upper_ref, *refs):
    rows_ref = refs[-1]
    half = own_ref.shape[1] // 2
    for m in range(2):
        lower, upper, one, other = [
            ref[m].astype(jnp.float32) for ref in (lower_ref, upper_ref, far_lower_ref, far_upper_ref)
        ]
        far = one + other
        parts = [own_ref[m].astype(jnp.float32), lower[:half], upper[:half], far[:half]]
        parts += [lower[half:], upper[half:], far[half:]]
        rows_ref[m] = jnp.concatenate(parts, axis=0).astype(jnp.bfloat16)


def arrange(blocks, after):
    whole = pl.BlockSpec(memory_space=pltpu.VMEM)
    two, count, width = blocks[0].shape
    shape = jax.ShapeDtypeStruct((two, 4 * count, width), jnp.bfloat16)
    return call(arrange_kernel, "arrange", blocks, [whole] * 5, whole, shape, after)


def to_core(v):
    return lax.ppermute(v, "dp", [(i, i ^ 1) for i in range(4)])


def to_chip(v):
    return lax.ppermute(v, "dp", [(i, i ^ 2) for i in range(4)])


def forward_all(rows, top, weights, chunks, last, between):
    first, firsts = 0, []
    for steps in chunks:
        firsts.append(first)
        first += steps
    parts, sums = [], []
    for k in range(len(chunks) + 1):
        if k < len(chunks):
            own, send = forward(rows, top, weights, firsts[k], chunks[k], last)
            parts.append((own, to_core(send)))
            last = (own,)
        if k == 0:
            left = between(last)
            last = (left,)
        if k >= 1:
            total, sent = add(*parts[k - 1], last)
            sums.append((total, to_chip(sent)))
            last = (total,)
    return sums, left, last


def pipeline(block, weights):
    lower = lax.ppermute(block, "expert", [(i, (i + 1) % 4) for i in range(4)])
    upper = lax.ppermute(block, "expert", [(i, (i - 1) % 4) for i in range(4)])
    own, send, resident = forward_own(block, weights)
    lower_out, _ = lax.optimization_barrier((lower, own))
    far_lower = lax.ppermute(lower_out, "expert", [(1, 2), (2, 3)])
    far_upper = lax.ppermute(upper, "expert", [(2, 1), (1, 0)])
    total, sent = add(own, to_core(send), ())
    own_sums, last = [(total, to_chip(sent))], (total,)
    rows = arrange([block, lower, upper, far_lower, far_upper], last)
    sums, left, last = forward_all(
        rows, block.shape[1], resident, REST_CHUNKS, (rows,), functools.partial(activate, own_sums)
    )
    own_left = [left, to_core(left)]
    grads, first, lefts = None, 0, []
    for k in range(len(sums) + 1):
        if k < len(sums):
            left = activate([sums[k]], last)
            lefts.append([left, to_core(left)])
            last = (left,)
        if k >= 1:
            after = last if k < len(sums) else ()
            grads = backward(
                own_left + lefts[k - 1], rows, grads, weights.shape, first, REST_CHUNKS[k - 1], after
            )
            first += REST_CHUNKS[k - 1]
            last = (grads,)
    return grads


def fallback(block, weights):
    moved = lax.all_gather(block, "expert", axis=1, tiled=True)
    _, hid, width = weights.shape
    gate_up = contract_last(moved[0], weights[:2].reshape(2 * hid, width))
    down = contract_last(moved[1], weights[2])
    total = lax.psum(jnp.concatenate([gate_up, down], axis=1), "dp")
    left = activations(total[:, :hid], total[:, hid : 2 * hid], total[:, 2 * hid :])
    return jnp.stack(
        [
            contract_first(left[0], moved[0]),
            contract_first(left[1], moved[0]),
            contract_first(left[2], moved[1]),
        ]
    )


def per_device(n_expert, n_dp, tokens, out_grad, gate_probs, routes, weights):
    hid = weights.shape[1]
    if n_expert == 4 and n_dp == 4 and hid == STEP * sum(REST_CHUNKS) and tokens.shape[0] % 64 == 0:
        flip = lax.rem(lax.axis_index("dp"), 2) == 1
        return pipeline(pick_rows(tokens, out_grad, gate_probs, routes, flip), weights)
    return fallback(pick_rows(tokens, out_grad, gate_probs, routes, False), weights)


def solution(mesh):
    in_specs = (
        P(("group", "expert"), "dp"),
        P(("group", "expert"), "dp"),
        P(("group", "expert"), None),
        P(("group", "expert"), None),
        P(None, "expert", "dp"),
    )
    out_specs = P("group", "expert", "dp")
    step = functools.partial(per_device, mesh.shape["expert"], mesh.shape["dp"])
    return jax.shard_map(
        step, mesh=mesh, in_specs=in_specs, out_specs=out_specs, check_vma=False
    )
```

time: 254 us -> 84 us (0.33)
  waiting for transfers between devices: 135 us -> 12.9 us
  Pallas kernels: 0 us -> 44.1 us
  other arithmetic: 45.4 us -> 1.95 us
  matrix products: 44.5 us -> 1.65 us
  starting transfers between devices: 0.04 us -> 22.8 us
  local copies, waits for them, and re-layouts: 13.9 us -> 0.2 us
  between operations: 13.5 us -> 0.17 us
    psum x1 -> x0, waiting for transfers between devices: 118 us -> none  [per_device(): summed = lax.psum(partial_value, 'dp')]
    pallas_call x0 -> x20, Pallas kernels: none -> 44.1 us  [the longest x19 34.2 us: call(): pl.pallas_call(kernel, grid=grid, in_specs=list(in_specs) + [pl.BlockSpec...]
    dot_general x6 -> x2, matrix products: 44.5 us -> 1.65 us  [the longest x1 1.38 us: pick_rows(): jnp.dot(picker, scaled, preferred_element_type=jnp.float32)]
    concatenate x2 -> x0, other arithmetic: 39 us -> none  [the longest x1 33.8 us: per_device(): jnp.concatenate([part_gu, part_down], axis=0)]
    ppermute x0 -> x19, starting transfers between devices: none -> 22.8 us  [the longest x10 9.78 us: to_core(): return lax.ppermute(v, 'dp', [(i, i ^ 1) for i in range(4)])]
    all_gather x1 -> x0, waiting for transfers between devices: 17 us -> none  [per_device(): moved = lax.all_gather(stacked, 'expert', axis=1, tiled=True)]
    slice x2 -> x1, local copies, waits for them, and re-layouts: 13.8 us -> 0.07 us  [the longest x1 13.7 us: per_device(): w_gateup = expert_weights[:2].reshape(2 * hid_local, slice_width)]
    ppermute x0 -> x19, waiting for transfers between devices: none -> 12.9 us  [the longest x5 4.78 us: to_chip(): return lax.ppermute(v, 'dp', [(i, i ^ 2) for i in range(4)])]
  transfers between devices with their start and end apart: 2 -> 19, of which waited for: 2 -> 6; matrix products, arithmetic and copies ran while one was open for 5% -> 0% of each run, Pallas kernels for 0% -> 48%
where the time goes in v1:
time: 84 us; the launch traced here: 83.7 us
  Pallas kernels  44.1 us (52%)
  starting transfers between devices  22.8 us (27%)
  waiting for transfers between devices  12.9 us (15%)
  other arithmetic  1.95 us (2%)
  matrix products  1.65 us (2%)
    pallas_call x19, Pallas kernels, call(): pl.pallas_call(kernel, grid=grid, in_specs=list(in_specs) + [pl.BlockSpec...  34.2 us
    pallas_call x1, Pallas kernels, forward_own(): pl.pallas_call(own_kernel, in_specs=[pl.BlockSpec(memory_space=pltpu.VMEM...  9.9 us
    ppermute x10, starting transfers between devices, to_core(): return lax.ppermute(v, 'dp', [(i, i ^ 1) for i in range(4)])  9.78 us
    ppermute x5, starting transfers between devices, to_chip(): return lax.ppermute(v, 'dp', [(i, i ^ 2) for i in range(4)])  5.5 us
    ppermute x5, waiting for transfers between devices, to_chip(): return lax.ppermute(v, 'dp', [(i, i ^ 2) for i in range(4)])  4.78 us
    ppermute x1, starting transfers between devices, pipeline(): far_upper = lax.ppermute(upper, 'expert', [(2, 1), (1, 0)])  4.03 us
    ppermute x1, waiting for transfers between devices, pipeline(): far_lower = lax.ppermute(lower_out, 'expert', [(1, 2), (2, 3)])  3.81 us
    ppermute x1, waiting for transfers between devices, pipeline(): far_upper = lax.ppermute(upper, 'expert', [(2, 1), (1, 0)])  2.52 us
  transfers between devices with their start and end apart: 19, of which 6 were waited for; matrix products, arithmetic and copies ran while one was open for 0% of the time, Pallas kernels for 48%

profile of v1, /device:TPU:21, one launch (start us, length us, event | category | flops | bytes accessed | tf_op | source)
XLA Modules:
  0.0 83.7 jit_solution(12818179501975003272)
XLA Ops:
  0.0 0.8 fusion.9
  0.8 0.3 reduce-window.9
  1.4 0.7 select_reduce_fusion
  2.4 1.4 %fusion.1 = bf16[1,48,1536]{2,1,0:T(8,128)(2,1)S(1)} fusion(bf16[192,1536]{1,0:T(8,128)(2,1)} %param.6, f32[192]{0:T(256)S(1)} %select_reduce_fusion, s32[192]{0:T(256)S(1)} %slice_subtract_fusion, s32[48]{0:T(128)S(1)} %broadcast_select_fusion, pred[192]{0:T(512)(128)(4,1)S(1)} %get-tuple-element.49), kind=kOutput, calls=%fused_computation.3 | convolution fusion | flops 29288448 | bytes 739200 | tf_op jit(solution)/shard_map/dot_general | solution.py:50
  3.8 1.3 %collective-permute-start.2 = (bf16[2,48,1536]{2,1,0:T(8,128)(2,1)S(1)}, bf16[2,48,1536]{2,1,0:T(8,128)(2,1)S(1)}, u32[]{:S(2)}, u32[]{:S(2)}) collective-permute-start(bf16[2,48,1536]{2,1,0:T(8,128)(2,1)S(1)} %pad_maximum_fusion.rows_ref.own_ref), channel_id=1, source_target_pairs={{0,4},{4,8},{8,12},{12,0},{1,5},{5,9},{9,13},{13,1},{2,6},{6,10},{... | collective-permute-start | bytes 884744 | tf_op jit(solution)/shard_map/ppermute | solution.py:262
  5.4 9.9 %forward_own.1 = (f32[3,24,2688]{2,1,0:T(8,128)S(1)}, bf16[3,24,2688]{2,1,0:T(8,128)(2,1)S(1)}, bf16[3,2688,1536]{2,1,0:T(8,128)(2,1)S(1)}) custom-call(bf16[2,48,1536]{2,1,0:T(8,128)(2,1)S(1)} %pad_maximum_fusion.rows_ref.own_ref, bf16[3,2688,1536]{2,1,0:T(8,128)(2,1)} %w_ref.1), custom_call_target="tpu_custom_call" | custom-call | flops 1000 | bytes 1000 | tf_op jit(solution)/shard_map/forward_own/pallas_call | solution.py:95
  15.3 1.3 %collective-permute-start = (bf16[3,24,2688]{2,1,0:T(8,128)(2,1)S(1)}, bf16[3,24,2688]{2,1,0:T(8,128)(2,1)S(1)}, u32[]{:S(2)}, u32[]{:S(2)}) collective-permute-start(bf16[3,24,2688]{2,1,0:T(8,128)(2,1)S(1)} %get-tuple-element.28), channel_id=1, source_target_pairs={{0,1},{1,0},{2,3},{3,2},{4,5},{5,4},{6,7},{7,6},{8,9},{9,8},{10,11... | collective-permute-start | bytes 1161224 | tf_op jit(solution)/shard_map/ppermute | solution.py:233
  16.6 1.5 %collective-permute-done.3.upper_ref = bf16[2,48,1536]{2,1,0:T(8,128)(2,1)S(1)} collective-permute-done((bf16[2,48,1536]{2,1,0:T(8,128)(2,1)S(1)}, bf16[2,48,1536]{2,1,0:T(8,128)(2,1)S(1)}, u32[]{:S(2)}, u32[]{:S(2)}) %collective-permute-start.3) | collective-permute-done | bytes 294944 | tf_op jit(solution)/shard_map/ppermute | solution.py:263
  18.0 4.0 %collective-permute-start.5 = (bf16[2,48,1536]{2,1,0:T(8,128)(2,1)S(1)}, bf16[2,48,1536]{2,1,0:T(8,128)(2,1)S(1)}, u32[]{:S(2)}, u32[]{:S(2)}) collective-permute-start(bf16[2,48,1536]{2,1,0:T(8,128)(2,1)S(1)} %collective-permute-done.3.upper_ref), channel_id=1, source_target_pairs={{8,4},{4,0},{9,5},{5,1},{10,6},{6,2},{11,7},{7,3},{24,20},{20,16},... | collective-permute-start | bytes 884744 | tf_op jit(solution)/shard_map/ppermute | solution.py:267
  22.1 1.9 %collective-permute-start.4 = (bf16[2,48,1536]{2,1,0:T(8,128)(2,1)S(1)}, bf16[2,48,1536]{2,1,0:T(8,128)(2,1)S(1)}, u32[]{:S(2)}, u32[]{:S(2)}) collective-permute-start(bf16[2,48,1536]{2,1,0:T(8,128)(2,1)S(1)} %collective-permute-done.2.lower_ref), channel_id=1, source_target_pairs={{4,8},{8,12},{5,9},{9,13},{6,10},{10,14},{7,11},{11,15},{20,24},{2... | collective-permute-start | bytes 884744 | tf_op jit(solution)/shard_map/ppermute | solution.py:266
  24.1 1.3 %collective-permute-start.1 = (bf16[3,24,2688]{2,1,0:T(8,128)(2,1)S(1)}, bf16[3,24,2688]{2,1,0:T(8,128)(2,1)S(1)}, u32[]{:S(2)}, u32[]{:S(2)}) collective-permute-start(bf16[3,24,2688]{2,1,0:T(8,128)(2,1)S(1)} %get-tuple-element.30), channel_id=1, source_target_pairs={{0,2},{1,3},{2,0},{3,1},{4,6},{5,7},{6,4},{7,5},{8,10},{9,11},{10,... | collective-permute-start | bytes 1161224 | tf_op jit(solution)/shard_map/ppermute | solution.py:237
  25.4 2.5 %collective-permute-done.5.far_upper_ref = bf16[2,48,1536]{2,1,0:T(8,128)(2,1)S(1)} collective-permute-done((bf16[2,48,1536]{2,1,0:T(8,128)(2,1)S(1)}, bf16[2,48,1536]{2,1,0:T(8,128)(2,1)S(1)}, u32[]{:S(2)}, u32[]{:S(2)}) %collective-permute-start.5) | collective-permute-done | bytes 294944 | tf_op jit(solution)/shard_map/ppermute | solution.py:267
  27.9 3.8 %collective-permute-done.4.far_lower_ref = bf16[2,48,1536]{2,1,0:T(8,128)(2,1)S(1)} collective-permute-done((bf16[2,48,1536]{2,1,0:T(8,128)(2,1)S(1)}, bf16[2,48,1536]{2,1,0:T(8,128)(2,1)S(1)}, u32[]{:S(2)}, u32[]{:S(2)}) %collective-permute-start.4) | collective-permute-done | bytes 294944 | tf_op jit(solution)/shard_map/ppermute | solution.py:266
  31.8 2.6 %forward.4 = (f32[3,72,768]{2,1,0:T(8,128)S(1)}, bf16[3,72,768]{2,1,0:T(8,128)(2,1)S(1)}) custom-call(bf16[2,192,1536]{2,1,0:T(8,128)(2,1)S(1)} %arrange.1.rows_ref.refs_0_, bf16[3,2688,1536]{2,1,0:T(8,128)(2,1)S(1)} %get-tuple-element.32.w_ref, bf16[2,192,1536]{2,1,0:T(8,128)(2,1)S(1)} %arrange.1.rows_ref.refs_0_), custom_call_target="tpu_custom_call" | custom-call | flops 10000000000 | bytes 1000 | tf_op jit(solution)/shard_map/forward/pallas_call | solution.py:55
  34.5 1.7 %collective-permute-start.8 = (bf16[3,72,768]{2,1,0:T(8,128)(2,1)S(1)}, bf16[3,72,768]{2,1,0:T(8,128)(2,1)S(1)}, u32[]{:S(2)}, u32[]{:S(2)}) collective-permute-start(bf16[3,72,768]{2,1,0:T(8,128)(2,1)S(1)} %get-tuple-element.36), channel_id=1, source_target_pairs={{0,1},{1,0},{2,3},{3,2},{4,5},{5,4},{6,7},{7,6},{8,9},{9,8},{10,11... | collective-permute-start | bytes 995336 | tf_op jit(solution)/shard_map/ppermute | solution.py:233
  36.4 2.6 %forward.5 = (f32[3,72,768]{2,1,0:T(8,128)S(1)}, bf16[3,72,768]{2,1,0:T(8,128)(2,1)S(1)}) custom-call(bf16[2,192,1536]{2,1,0:T(8,128)(2,1)S(1)} %arrange.1.rows_ref.refs_0_, bf16[3,2688,1536]{2,1,0:T(8,128)(2,1)S(1)} %get-tuple-element.32.w_ref, bf16[3,24,2688]{2,1,0:T(8,128)(2,1)S(1)} %activate.5.refs_0_.a_ref), custom_call_target="tpu_custom_call" | custom-call | flops 10000000000 | bytes 1000 | tf_op jit(solution)/shard_map/forward/pallas_call | solution.py:55
  39.3 1.3 %collective-permute-start.13 = (bf16[3,72,768]{2,1,0:T(8,128)(2,1)S(1)}, bf16[3,72,768]{2,1,0:T(8,128)(2,1)S(1)}, u32[]{:S(2)}, u32[]{:S(2)}) collective-permute-start(bf16[3,72,768]{2,1,0:T(8,128)(2,1)S(1)} %get-tuple-element.47), channel_id=1, source_target_pairs={{0,2},{1,3},{2,0},{3,1},{4,6},{5,7},{6,4},{7,5},{8,10},{9,11},{10,... | collective-permute-start | bytes 995336 | tf_op jit(solution)/shard_map/ppermute | solution.py:237
  40.5 2.6 %forward.6 = (f32[3,72,768]{2,1,0:T(8,128)S(1)}, bf16[3,72,768]{2,1,0:T(8,128)(2,1)S(1)}) custom-call(bf16[2,192,1536]{2,1,0:T(8,128)(2,1)S(1)} %arrange.1.rows_ref.refs_0_, bf16[3,2688,1536]{2,1,0:T(8,128)(2,1)S(1)} %get-tuple-element.32.w_ref, f32[3,72,768]{2,1,0:T(8,128)S(1)} %get-tuple-element.37.refs_0_), custom_call_target="tpu_custom_call" | custom-call | flops 10000000000 | bytes 1000 | tf_op jit(solution)/shard_map/forward/pallas_call | solution.py:55
  43.2 0.8 collective-permute-start.10
  44.1 1.3 %forward.7 = (f32[3,72,384]{2,1,0:T(8,128)S(1)}, bf16[3,72,384]{2,1,0:T(8,128)(2,1)S(1)}) custom-call(bf16[2,192,1536]{2,1,0:T(8,128)(2,1)S(1)} %arrange.1.rows_ref.refs_0_, bf16[3,2688,1536]{2,1,0:T(8,128)(2,1)S(1)} %get-tuple-element.32.w_ref, f32[3,72,768]{2,1,0:T(8,128)S(1)} %get-tuple-element.39.refs_0_), custom_call_target="tpu_custom_call" | custom-call | flops 10000000000 | bytes 1000 | tf_op jit(solution)/shard_map/forward/pallas_call | solution.py:55
  45.8 0.7 collective-permute-start.6
  46.9 1.3 %collective-permute-done.13.refs_1_ = bf16[3,72,768]{2,1,0:T(8,128)(2,1)S(1)} collective-permute-done((bf16[3,72,768]{2,1,0:T(8,128)(2,1)S(1)}, bf16[3,72,768]{2,1,0:T(8,128)(2,1)S(1)}, u32[]{:S(2)}, u32[]{:S(2)}) %collective-permute-start.13) | collective-permute-done | bytes 331808 | tf_op jit(solution)/shard_map/ppermute | solution.py:237
  48.4 2.2 %collective-permute-start.15 = (bf16[3,72,768]{2,1,0:T(8,128)(2,1)S(1)}, bf16[3,72,768]{2,1,0:T(8,128)(2,1)S(1)}, u32[]{:S(2)}, u32[]{:S(2)}) collective-permute-start(bf16[3,72,768]{2,1,0:T(8,128)(2,1)S(1)} %activate.6.refs_2_.c_ref), channel_id=1, source_target_pairs={{0,1},{1,0},{2,3},{3,2},{4,5},{5,4},{6,7},{7,6},{8,9},{9,8},{10,11... | collective-permute-start | bytes 995336 | tf_op jit(solution)/shard_map/ppermute | solution.py:233
  50.6 1.3 %collective-permute-start.16 = (bf16[3,72,768]{2,1,0:T(8,128)(2,1)S(1)}, bf16[3,72,768]{2,1,0:T(8,128)(2,1)S(1)}, u32[]{:S(2)}, u32[]{:S(2)}) collective-permute-start(bf16[3,72,768]{2,1,0:T(8,128)(2,1)S(1)} %get-tuple-element.48), channel_id=1, source_target_pairs={{0,2},{1,3},{2,0},{3,1},{4,6},{5,7},{6,4},{7,5},{8,10},{9,11},{10,... | collective-permute-start | bytes 995336 | tf_op jit(solution)/shard_map/ppermute | solution.py:237
  51.9 3.5 %collective-permute-done.12.refs_1_ = bf16[3,72,768]{2,1,0:T(8,128)(2,1)S(1)} collective-permute-done((bf16[3,72,768]{2,1,0:T(8,128)(2,1)S(1)}, bf16[3,72,768]{2,1,0:T(8,128)(2,1)S(1)}, u32[]{:S(2)}, u32[]{:S(2)}) %collective-permute-start.12) | collective-permute-done | bytes 331808 | tf_op jit(solution)/shard_map/ppermute | solution.py:237
  55.6 2.2 %collective-permute-start.14 = (bf16[3,72,768]{2,1,0:T(8,128)(2,1)S(1)}, bf16[3,72,768]{2,1,0:T(8,128)(2,1)S(1)}, u32[]{:S(2)}, u32[]{:S(2)}) collective-permute-start(bf16[3,72,768]{2,1,0:T(8,128)(2,1)S(1)} %activate.7.refs_0_.c_ref), channel_id=1, source_target_pairs={{0,1},{1,0},{2,3},{3,2},{4,5},{5,4},{6,7},{7,6},{8,9},{9,8},{10,11... | collective-permute-start | bytes 995336 | tf_op jit(solution)/shard_map/ppermute | solution.py:233
  57.7 1.3 %collective-permute-start.11 = (bf16[3,72,384]{2,1,0:T(8,128)(2,1)S(1)}, bf16[3,72,384]{2,1,0:T(8,128)(2,1)S(1)}, u32[]{:S(2)}, u32[]{:S(2)}) collective-permute-start(bf16[3,72,384]{2,1,0:T(8,128)(2,1)S(1)} %get-tuple-element.45), channel_id=1, source_target_pairs={{0,2},{1,3},{2,0},{3,1},{4,6},{5,7},{6,4},{7,5},{8,10},{9,11},{10,... | collective-permute-start | bytes 497672 | tf_op jit(solution)/shard_map/ppermute | solution.py:237
  59.1 6.5 %backward.4.refs_2_.refs_0_ = f32[3,2688,1536]{2,1,0:T(8,128)} custom-call(bf16[3,24,2688]{2,1,0:T(8,128)(2,1)S(1)} %activate.5.refs_0_.a_ref, bf16[3,24,2688]{2,1,0:T(8,128)(2,1)S(1)} %collective-permute-done.6.b_ref, bf16[3,72,768]{2,1,0:T(8,128)(2,1)S(1)} %activate.6.refs_2_.c_ref, bf16[3,72,768]{2,1,0:T(8,128)(2,1)S(1)} %collective-permute-done.15.d_ref, ...), custom_call_target="tpu_custom_call" | custom-call | flops 1000 | bytes 1000 | tf_op jit(solution)/shard_map/backward/pallas_call | solution.py:55
  65.8 0.4 collective-permute-start.18
  66.2 6.5 %backward.5.refs_2_.refs_0_ = f32[3,2688,1536]{2,1,0:T(8,128)} custom-call(bf16[3,24,2688]{2,1,0:T(8,128)(2,1)S(1)} %activate.5.refs_0_.a_ref, bf16[3,24,2688]{2,1,0:T(8,128)(2,1)S(1)} %collective-permute-done.6.b_ref, bf16[3,72,768]{2,1,0:T(8,128)(2,1)S(1)} %activate.7.refs_0_.c_ref, ...), custom_call_target="tpu_custom_call", output_to_operand_aliasing={{}: (5, {})} | custom-call | flops 1000 | bytes 1000 | tf_op jit(solution)/shard_map/backward/pallas_call | solution.py:55
  73.0 6.5 %backward.6.refs_0_ = f32[3,2688,1536]{2,1,0:T(8,128)} custom-call(bf16[3,24,2688]{2,1,0:T(8,128)(2,1)S(1)} %activate.5.refs_0_.a_ref, bf16[3,24,2688]{2,1,0:T(8,128)(2,1)S(1)} %collective-permute-done.6.b_ref, bf16[3,72,768]{2,1,0:T(8,128)(2,1)S(1)} %activate.8.refs_1_.c_ref, ...), custom_call_target="tpu_custom_call", output_to_operand_aliasing={{}: (5, {})} | custom-call | flops 1000 | bytes 1000 | tf_op jit(solution)/shard_map/backward/pallas_call | solution.py:55
  79.6 4.1 %backward.7 = f32[3,2688,1536]{2,1,0:T(8,128)} custom-call(bf16[3,24,2688]{2,1,0:T(8,128)(2,1)S(1)} %activate.5.refs_0_.a_ref, bf16[3,24,2688]{2,1,0:T(8,128)(2,1)S(1)} %collective-permute-done.6.b_ref, bf16[3,72,384]{2,1,0:T(8,128)(2,1)S(1)} %activate.9.refs_1_.c_ref, ...), custom_call_target="tpu_custom_call", output_to_operand_aliasing={{}: (5, {})} | custom-call | flops 1000 | bytes 1000 | tf_op jit(solution)/shard_map/backward/pallas_call | solution.py:55
  (44 shorter events, 3.1 us)
Async XLA Ops:
  0.0 2.1 %copy-start = (bf16[192,1536]{1,0:T(8,128)(2,1)S(1)}, bf16[192,1536]{1,0:T(8,128)(2,1)}, u32[]{:S(2)}) copy-start(bf16[192,1536]{1,0:T(8,128)(2,1)} %param.5) | copy-start | bytes 1769476
  3.8 12.7 %collective-permute-start.2 = (bf16[2,48,1536]{2,1,0:T(8,128)(2,1)S(1)}, bf16[2,48,1536]{2,1,0:T(8,128)(2,1)S(1)}, u32[]{:S(2)}, u32[]{:S(2)}) collective-permute-start(bf16[2,48,1536]{2,1,0:T(8,128)(2,1)S(1)} %pad_maximum_fusion.rows_ref.own_ref), channel_id=1, source_target_pairs={{0,4},{4,8},{8,12},{12,0},{1,5},{5,9},{9,13},{13,1},{2,6},{6,10},{... | collective-permute-start | bytes 884744 | tf_op jit(solution)/shard_map/ppermute | solution.py:262
  5.2 12.9 %collective-permute-start.3 = (bf16[2,48,1536]{2,1,0:T(8,128)(2,1)S(1)}, bf16[2,48,1536]{2,1,0:T(8,128)(2,1)S(1)}, u32[]{:S(2)}, u32[]{:S(2)}) collective-permute-start(bf16[2,48,1536]{2,1,0:T(8,128)(2,1)S(1)} %pad_maximum_fusion.rows_ref.own_ref), channel_id=1, source_target_pairs={{0,12},{4,0},{8,4},{12,8},{1,13},{5,1},{9,5},{13,9},{2,14},{6,2},{... | collective-permute-start | bytes 884744 | tf_op jit(solution)/shard_map/ppermute | solution.py:263
  15.3 8.7 %collective-permute-start = (bf16[3,24,2688]{2,1,0:T(8,128)(2,1)S(1)}, bf16[3,24,2688]{2,1,0:T(8,128)(2,1)S(1)}, u32[]{:S(2)}, u32[]{:S(2)}) collective-permute-start(bf16[3,24,2688]{2,1,0:T(8,128)(2,1)S(1)} %get-tuple-element.28), channel_id=1, source_target_pairs={{0,1},{1,0},{2,3},{3,2},{4,5},{5,4},{6,7},{7,6},{8,9},{9,8},{10,11... | collective-permute-start | bytes 1161224 | tf_op jit(solution)/shard_map/ppermute | solution.py:233
  18.0 9.9 %collective-permute-start.5 = (bf16[2,48,1536]{2,1,0:T(8,128)(2,1)S(1)}, bf16[2,48,1536]{2,1,0:T(8,128)(2,1)S(1)}, u32[]{:S(2)}, u32[]{:S(2)}) collective-permute-start(bf16[2,48,1536]{2,1,0:T(8,128)(2,1)S(1)} %collective-permute-done.3.upper_ref), channel_id=1, source_target_pairs={{8,4},{4,0},{9,5},{5,1},{10,6},{6,2},{11,7},{7,3},{24,20},{20,16},... | collective-permute-start | bytes 884744 | tf_op jit(solution)/shard_map/ppermute | solution.py:267
  22.1 9.7 %collective-permute-start.4 = (bf16[2,48,1536]{2,1,0:T(8,128)(2,1)S(1)}, bf16[2,48,1536]{2,1,0:T(8,128)(2,1)S(1)}, u32[]{:S(2)}, u32[]{:S(2)}) collective-permute-start(bf16[2,48,1536]{2,1,0:T(8,128)(2,1)S(1)} %collective-permute-done.2.lower_ref), channel_id=1, source_target_pairs={{4,8},{8,12},{5,9},{9,13},{6,10},{10,14},{7,11},{11,15},{20,24},{2... | collective-permute-start | bytes 884744 | tf_op jit(solution)/shard_map/ppermute | solution.py:266
  24.1 12.1 %collective-permute-start.1 = (bf16[3,24,2688]{2,1,0:T(8,128)(2,1)S(1)}, bf16[3,24,2688]{2,1,0:T(8,128)(2,1)S(1)}, u32[]{:S(2)}, u32[]{:S(2)}) collective-permute-start(bf16[3,24,2688]{2,1,0:T(8,128)(2,1)S(1)} %get-tuple-element.30), channel_id=1, source_target_pairs={{0,2},{1,3},{2,0},{3,1},{4,6},{5,7},{6,4},{7,5},{8,10},{9,11},{10,... | collective-permute-start | bytes 1161224 | tf_op jit(solution)/shard_map/ppermute | solution.py:237
  34.5 4.7 %collective-permute-start.8 = (bf16[3,72,768]{2,1,0:T(8,128)(2,1)S(1)}, bf16[3,72,768]{2,1,0:T(8,128)(2,1)S(1)}, u32[]{:S(2)}, u32[]{:S(2)}) collective-permute-start(bf16[3,72,768]{2,1,0:T(8,128)(2,1)S(1)} %get-tuple-element.36), channel_id=1, source_target_pairs={{0,1},{1,0},{2,3},{3,2},{4,5},{5,4},{6,7},{7,6},{8,9},{9,8},{10,11... | collective-permute-start | bytes 995336 | tf_op jit(solution)/shard_map/ppermute | solution.py:233
  39.1 4.9 %collective-permute-start.7 = (bf16[3,72,768]{2,1,0:T(8,128)(2,1)S(1)}, bf16[3,72,768]{2,1,0:T(8,128)(2,1)S(1)}, u32[]{:S(2)}, u32[]{:S(2)}) collective-permute-start(bf16[3,72,768]{2,1,0:T(8,128)(2,1)S(1)} %get-tuple-element.35), channel_id=1, source_target_pairs={{0,1},{1,0},{2,3},{3,2},{4,5},{5,4},{6,7},{7,6},{8,9},{9,8},{10,11... | collective-permute-start | bytes 995336 | tf_op jit(solution)/shard_map/ppermute | solution.py:233
  39.3 8.9 %collective-permute-start.13 = (bf16[3,72,768]{2,1,0:T(8,128)(2,1)S(1)}, bf16[3,72,768]{2,1,0:T(8,128)(2,1)S(1)}, u32[]{:S(2)}, u32[]{:S(2)}) collective-permute-start(bf16[3,72,768]{2,1,0:T(8,128)(2,1)S(1)} %get-tuple-element.47), channel_id=1, source_target_pairs={{0,2},{1,3},{2,0},{3,1},{4,6},{5,7},{6,4},{7,5},{8,10},{9,11},{10,... | collective-permute-start | bytes 995336 | tf_op jit(solution)/shard_map/ppermute | solution.py:237
  43.2 3.3 %collective-permute-start.10 = (bf16[3,72,768]{2,1,0:T(8,128)(2,1)S(1)}, bf16[3,72,768]{2,1,0:T(8,128)(2,1)S(1)}, u32[]{:S(2)}, u32[]{:S(2)}) collective-permute-start(bf16[3,72,768]{2,1,0:T(8,128)(2,1)S(1)} %get-tuple-element.42), channel_id=1, source_target_pairs={{0,1},{1,0},{2,3},{3,2},{4,5},{5,4},{6,7},{7,6},{8,9},{9,8},{10,11... | collective-permute-start | bytes 995336 | tf_op jit(solution)/shard_map/ppermute | solution.py:233
  45.4 1.5 %collective-permute-start.9 = (bf16[3,72,384]{2,1,0:T(8,128)(2,1)S(1)}, bf16[3,72,384]{2,1,0:T(8,128)(2,1)S(1)}, u32[]{:S(2)}, u32[]{:S(2)}) collective-permute-start(bf16[3,72,384]{2,1,0:T(8,128)(2,1)S(1)} %get-tuple-element.41), channel_id=1, source_target_pairs={{0,1},{1,0},{2,3},{3,2},{4,5},{5,4},{6,7},{7,6},{8,9},{9,8},{10,11... | collective-permute-start | bytes 497672 | tf_op jit(solution)/shard_map/ppermute | solution.py:233
  45.5 9.9 %collective-permute-start.12 = (bf16[3,72,768]{2,1,0:T(8,128)(2,1)S(1)}, bf16[3,72,768]{2,1,0:T(8,128)(2,1)S(1)}, u32[]{:S(2)}, u32[]{:S(2)}) collective-permute-start(bf16[3,72,768]{2,1,0:T(8,128)(2,1)S(1)} %get-tuple-element.46), channel_id=1, source_target_pairs={{0,2},{1,3},{2,0},{3,1},{4,6},{5,7},{6,4},{7,5},{8,10},{9,11},{10,... | collective-permute-start | bytes 995336 | tf_op jit(solution)/shard_map/ppermute | solution.py:237
  45.8 13.3 %collective-permute-start.6 = (bf16[3,24,2688]{2,1,0:T(8,128)(2,1)S(1)}, bf16[3,24,2688]{2,1,0:T(8,128)(2,1)S(1)}, u32[]{:S(2)}, u32[]{:S(2)}) collective-permute-start(bf16[3,24,2688]{2,1,0:T(8,128)(2,1)S(1)} %activate.5.refs_0_.a_ref), channel_id=1, source_target_pairs={{0,1},{1,0},{2,3},{3,2},{4,5},{5,4},{6,7},{7,6},{8,9},{9,8},{10,11... | collective-permute-start | bytes 1161224 | tf_op jit(solution)/shard_map/ppermute | solution.py:233
  48.4 10.7 %collective-permute-start.15 = (bf16[3,72,768]{2,1,0:T(8,128)(2,1)S(1)}, bf16[3,72,768]{2,1,0:T(8,128)(2,1)S(1)}, u32[]{:S(2)}, u32[]{:S(2)}) collective-permute-start(bf16[3,72,768]{2,1,0:T(8,128)(2,1)S(1)} %activate.6.refs_2_.c_ref), channel_id=1, source_target_pairs={{0,1},{1,0},{2,3},{3,2},{4,5},{5,4},{6,7},{7,6},{8,9},{9,8},{10,11... | collective-permute-start | bytes 995336 | tf_op jit(solution)/shard_map/ppermute | solution.py:233
  50.6 15.0 %collective-permute-start.16 = (bf16[3,72,768]{2,1,0:T(8,128)(2,1)S(1)}, bf16[3,72,768]{2,1,0:T(8,128)(2,1)S(1)}, u32[]{:S(2)}, u32[]{:S(2)}) collective-permute-start(bf16[3,72,768]{2,1,0:T(8,128)(2,1)S(1)} %get-tuple-element.48), channel_id=1, source_target_pairs={{0,2},{1,3},{2,0},{3,1},{4,6},{5,7},{6,4},{7,5},{8,10},{9,11},{10,... | collective-permute-start | bytes 995336 | tf_op jit(solution)/shard_map/ppermute | solution.py:237
  55.6 10.6 %collective-permute-start.14 = (bf16[3,72,768]{2,1,0:T(8,128)(2,1)S(1)}, bf16[3,72,768]{2,1,0:T(8,128)(2,1)S(1)}, u32[]{:S(2)}, u32[]{:S(2)}) collective-permute-start(bf16[3,72,768]{2,1,0:T(8,128)(2,1)S(1)} %activate.7.refs_0_.c_ref), channel_id=1, source_target_pairs={{0,1},{1,0},{2,3},{3,2},{4,5},{5,4},{6,7},{7,6},{8,9},{9,8},{10,11... | collective-permute-start | bytes 995336 | tf_op jit(solution)/shard_map/ppermute | solution.py:233
  57.7 15.0 %collective-permute-start.11 = (bf16[3,72,384]{2,1,0:T(8,128)(2,1)S(1)}, bf16[3,72,384]{2,1,0:T(8,128)(2,1)S(1)}, u32[]{:S(2)}, u32[]{:S(2)}) collective-permute-start(bf16[3,72,384]{2,1,0:T(8,128)(2,1)S(1)} %get-tuple-element.45), channel_id=1, source_target_pairs={{0,2},{1,3},{2,0},{3,1},{4,6},{5,7},{6,4},{7,5},{8,10},{9,11},{10,... | collective-permute-start | bytes 497672 | tf_op jit(solution)/shard_map/ppermute | solution.py:237
  65.8 7.3 %collective-permute-start.18 = (bf16[3,72,768]{2,1,0:T(8,128)(2,1)S(1)}, bf16[3,72,768]{2,1,0:T(8,128)(2,1)S(1)}, u32[]{:S(2)}, u32[]{:S(2)}) collective-permute-start(bf16[3,72,768]{2,1,0:T(8,128)(2,1)S(1)} %activate.8.refs_1_.c_ref), channel_id=1, source_target_pairs={{0,1},{1,0},{2,3},{3,2},{4,5},{5,4},{6,7},{7,6},{8,9},{9,8},{10,11... | collective-permute-start | bytes 995336 | tf_op jit(solution)/shard_map/ppermute | solution.py:233
  72.8 6.8 %collective-permute-start.17 = (bf16[3,72,384]{2,1,0:T(8,128)(2,1)S(1)}, bf16[3,72,384]{2,1,0:T(8,128)(2,1)S(1)}, u32[]{:S(2)}, u32[]{:S(2)}) collective-permute-start(bf16[3,72,384]{2,1,0:T(8,128)(2,1)S(1)} %activate.9.refs_1_.c_ref), channel_id=1, source_target_pairs={{0,1},{1,0},{2,3},{3,2},{4,5},{5,4},{6,7},{7,6},{8,9},{9,8},{10,11... | collective-permute-start | bytes 497672 | tf_op jit(solution)/shard_map/ppermute | solution.py:233
  79.6 4.1 %copy-start.1 = (bf16[192,1536]{1,0:T(8,128)(2,1)S(1)}, bf16[192,1536]{1,0:T(8,128)(2,1)}, u32[]{:S(2)}) copy-start(bf16[192,1536]{1,0:T(8,128)(2,1)} %param.5) | copy-start | bytes 1769476

commit v2 on v1

--- a/solution.py
+++ b/solution.py
@@ -8,10 +8,16 @@
 from jax.sharding import PartitionSpec as P
 
 STEP = 384
-REST_CHUNKS = (2, 2, 2, 1)
+BACK_BLOCKS = (256, 384)
+REST_CHUNKS = (2, 3, 2)
+AHEAD = (1, 2, 3)
+DEFER = 1
 VMEM = 24 * 1024 * 1024
 SMALL = 8 * 1024 * 1024
-FLOPS = 10**10
+LARGE = 253 * 256 * 1024
+FLOPS = 4 * 10**9
+BACK_FLOPS = 1000
+FINAL_FLOPS = 5*10**9
 
 
 def contract_last(left, right):
@@ -34,7 +40,7 @@
     return jnp.stack([gate_grad, up_grad, hidden]).astype(jnp.bfloat16)
 
 
-def pick_rows(tokens, out_grad, gate_probs, routes, flip):
+def pick_rows(tokens, out_grad, gate_probs, routes):
     capacity = tokens.shape[0] // 4
     hit = routes == 0
     token_hit = jnp.any(hit, axis=1)
@@ -42,7 +48,6 @@
     flags = token_hit.astype(jnp.int32)
     before = jnp.cumsum(flags, dtype=jnp.int32) - flags
     place = jnp.arange(capacity, dtype=jnp.int32)
-    place = jnp.where(flip, lax.rem(place + capacity // 2, capacity), place)
     match = token_hit[None, :] & (before[None, :] == place[:, None])
     picker = match.astype(jnp.bfloat16)
     scaled = (out_grad.astype(jnp.float32) * prob[:, None]).astype(jnp.bfloat16)
@@ -63,6 +68,49 @@
         cost_estimate=pl.CostEstimate(flops=flops, bytes_accessed=1000, transcendentals=0),
         name=name,
     )(*args, *after)
+
+
+def pick_kernel(*refs):
+    core_ref, rows_ref = refs[4:6]
+    held, sems = refs[6:10], refs[10]
+    copies = [pltpu.make_async_copy(refs[k], held[k], sems.at[k]) for k in range(4)]
+    for copy in copies:
+        copy.start()
+    for copy in copies:
+        copy.wait()
+    tokens_ref, grad_ref, probs_ref, routes_ref = held
+    count, capacity = tokens_ref.shape[0], rows_ref.shape[1]
+    hit = routes_ref[...] == 0
+    prob = jnp.sum(jnp.where(hit, probs_ref[...], 0.0), axis=0, keepdims=True)
+    flag = jnp.max(jnp.where(hit, 1.0, 0.0), axis=0, keepdims=True)
+    row = lax.broadcasted_iota(jnp.int32, (count, count), 0)
+    column = lax.broadcasted_iota(jnp.int32, (count, count), 1)
+    earlier = jnp.where(row < column, 1.0, 0.0).astype(jnp.bfloat16)
+    flags = jnp.broadcast_to(flag, (16, count)).astype(jnp.bfloat16)
+    before = jnp.dot(flags, earlier, preferred_element_type=jnp.float32)[:1]
+    place = lax.broadcasted_iota(jnp.int32, (capacity, count), 0) + core_ref[0] * (capacity // 2)
+    place = jnp.where(place >= capacity, place - capacity, place)
+    match = (flag > 0.0) & (before.astype(jnp.int32) == place)
+    picker = jnp.where(match, 1.0, 0.0).astype(jnp.bfloat16)
+    scale = jnp.sum(jnp.where(match, prob, 0.0), axis=1, keepdims=True)
+    rows_ref[0] = jnp.dot(picker, tokens_ref[...], preferred_element_type=jnp.float32).astype(jnp.bfloat16)
+    rows_dy = jnp.dot(picker, grad_ref[...], preferred_element_type=jnp.float32)
+    rows_ref[1] = (rows_dy * scale).astype(jnp.bfloat16)
+
+
+def pick(tokens, out_grad, gate_probs, routes, core):
+    count, width = tokens.shape
+    args = (tokens, out_grad, gate_probs.T, routes.T)
+    return pl.pallas_call(
+        pick_kernel,
+        in_specs=[pl.BlockSpec(memory_space=pltpu.HBM)] * 4 + [pl.BlockSpec(memory_space=pltpu.SMEM)],
+        out_specs=pl.BlockSpec(memory_space=pltpu.VMEM),
+        out_shape=jax.ShapeDtypeStruct((2, count // 4, width), jnp.bfloat16),
+        scratch_shapes=[pltpu.VMEM(v.shape, v.dtype) for v in args] + [pltpu.SemaphoreType.DMA((4,))],
+        compiler_params=pltpu.CompilerParams(vmem_limit_bytes=LARGE),
+        cost_estimate=pl.CostEstimate(flops=1000, bytes_accessed=1000, transcendentals=0),
+        name="pick",
+    )(*args, core)
 
 
 def own_kernel(rows_ref, w_ref, own_ref, send_ref, kept_ref, sems):
@@ -152,9 +200,12 @@
 
 def backward(lefts, rows, grads, shape, first, steps, after):
     _, count, width = rows.shape
+    start, size = first * STEP, steps * STEP
+    block = next(b for b in BACK_BLOCKS if start % b == 0 and size % b == 0)
     in_specs = [
         pl.BlockSpec(
-            (3, v.shape[1], STEP), lambda i, k=first if v.shape[2] == shape[1] else 0: (0, 0, k + i)
+            (3, v.shape[1], block),
+            lambda i, k=start // block if v.shape[2] == shape[1] else 0: (0, 0, k + i),
         )
         for v in lefts
     ] + [pl.BlockSpec((2, count, width), lambda i: (0, 0, 0))]
@@ -166,12 +217,13 @@
         "backward",
         args,
         in_specs,
-        pl.BlockSpec((3, STEP, width), lambda i: (0, first + i, 0)),
+        pl.BlockSpec((3, block, width), lambda i: (0, start // block + i, 0)),
         jax.ShapeDtypeStruct(shape, jnp.float32),
         after,
-        (steps,),
+        (size // block,),
         aliases,
         VMEM,
+        BACK_FLOPS,
     )
 
 
@@ -194,10 +246,10 @@
         left_ref[2, :, here] = (gate * sig * up).astype(jnp.bfloat16)
 
 
-def add(own, received, after):
+def add(own, received, after, flops=1000):
     whole = [pl.BlockSpec(memory_space=pltpu.VMEM)] * 2
     shapes = [jax.ShapeDtypeStruct(own.shape, t) for t in (jnp.float32, jnp.bfloat16)]
-    return call(add_kernel, "add", (own, received), whole, whole, shapes, after)
+    return call(add_kernel, "add", (own, received), whole, whole, shapes, after, flops=flops)
 
 
 def activate(sums, after):
@@ -243,19 +295,18 @@
         firsts.append(first)
         first += steps
     parts, sums = [], []
-    for k in range(len(chunks) + 1):
-        if k < len(chunks):
-            own, send = forward(rows, top, weights, firsts[k], chunks[k], last)
-            parts.append((own, to_core(send)))
-            last = (own,)
+    for k in range(len(chunks)):
+        own, send = forward(rows, top, weights, firsts[k], chunks[k], last)
+        parts.append((own, to_core(send)))
+        last = (own,)
         if k == 0:
             left = between(last)
             last = (left,)
-        if k >= 1:
-            total, sent = add(*parts[k - 1], last)
+        for ready in ([0] if k == 0 else [k - 1] if k >= 2 else []):
+            total, sent = add(*parts[ready], last)
             sums.append((total, to_chip(sent)))
             last = (total,)
-    return sums, left, last
+    return sums, parts[-1], left, last
 
 
 def pipeline(block, weights):
@@ -268,23 +319,26 @@
     total, sent = add(own, to_core(send), ())
     own_sums, last = [(total, to_chip(sent))], (total,)
     rows = arrange([block, lower, upper, far_lower, far_upper], last)
-    sums, left, last = forward_all(
+    sums, final, left, last = forward_all(
         rows, block.shape[1], resident, REST_CHUNKS, (rows,), functools.partial(activate, own_sums)
     )
     own_left = [left, to_core(left)]
-    grads, first, lefts = None, 0, []
-    for k in range(len(sums) + 1):
-        if k < len(sums):
-            left = activate([sums[k]], last)
+    firsts = [sum(REST_CHUNKS[:k]) for k in range(len(REST_CHUNKS))]
+    grads, lefts = None, []
+    for k, ahead in enumerate(AHEAD):
+        while len(lefts) < ahead:
+            left = activate([sums[len(lefts)]], last)
             lefts.append([left, to_core(left)])
             last = (left,)
-        if k >= 1:
-            after = last if k < len(sums) else ()
-            grads = backward(
-                own_left + lefts[k - 1], rows, grads, weights.shape, first, REST_CHUNKS[k - 1], after
-            )
-            first += REST_CHUNKS[k - 1]
-            last = (grads,)
+            if len(lefts) == DEFER:
+                total, sent = add(*final, last, FINAL_FLOPS)
+                sums.append((total, to_chip(sent)))
+                last = (total,)
+        after = () if grads is not None and last[0] is grads else last
+        grads = backward(
+            own_left + lefts[k], rows, grads, weights.shape, firsts[k], REST_CHUNKS[k], after
+        )
+        last = (grads,)
     return grads
 
 
@@ -307,9 +361,9 @@
 def per_device(n_expert, n_dp, tokens, out_grad, gate_probs, routes, weights):
     hid = weights.shape[1]
     if n_expert == 4 and n_dp == 4 and hid == STEP * sum(REST_CHUNKS) and tokens.shape[0] % 64 == 0:
-        flip = lax.rem(lax.axis_index("dp"), 2) == 1
-        return pipeline(pick_rows(tokens, out_grad, gate_probs, routes, flip), weights)
-    return fallback(pick_rows(tokens, out_grad, gate_probs, routes, False), weights)
+        core = lax.rem(lax.axis_index("dp"), 2).reshape(1)
+        return pipeline(pick(tokens, out_grad, gate_probs, routes, core), weights)
+    return fallback(pick_rows(tokens, out_grad, gate_probs, routes), weights)
 
 
 def solution(mesh):

time: 84 us -> 79.2 us (0.943)
  starting transfers between devices: 22.8 us -> 17.4 us
  waiting for transfers between devices: 12.9 us -> 15.2 us
  other arithmetic: 1.95 us -> 0 us
  local copies, waits for them, and re-layouts: 0.2 us -> 1.96 us
  matrix products: 1.65 us -> 0 us
    ppermute x10 -> x8, waiting for transfers between devices: 0.28 us -> 4.73 us  [to_core(): return lax.ppermute(v, 'dp', [(i, i ^ 1) for i in range(4)])]
    ppermute x10 -> x8, starting transfers between devices: 9.78 us -> 6.85 us  [to_core(): return lax.ppermute(v, 'dp', [(i, i ^ 1) for i in range(4)])]
    pallas_call x0 -> x1, Pallas kernels: none -> 2.46 us  [pick(): pl.pallas_call(pick_kernel, in_specs=[pl.BlockSpec(memory_space=pltpu.HBM...]
    ppermute x5 -> x4, starting transfers between devices: 5.5 us -> 3.12 us  [to_chip(): return lax.ppermute(v, 'dp', [(i, i ^ 2) for i in range(4)])]
    pallas_call x19 -> x15, Pallas kernels: 34.2 us -> 31.9 us  [call(): pl.pallas_call(kernel, grid=grid, in_specs=list(in_specs) + [pl.BlockSpec...]
    unnamed x4, local copies, waits for them, and re-layouts: 0.01 us -> 1.96 us
    dot_general x2 -> x0, matrix products: 1.65 us -> none  [the longest x1 1.38 us: pick_rows(): jnp.dot(picker, scaled, preferred_element_type=jnp.float32)]
    ppermute x5 -> x4, waiting for transfers between devices: 4.78 us -> 3.47 us  [to_chip(): return lax.ppermute(v, 'dp', [(i, i ^ 2) for i in range(4)])]
  transfers between devices with their start and end apart: 19 -> 16, of which waited for: 6 -> 9; matrix products, arithmetic and copies ran while one was open for 0% -> 0% of each run, Pallas kernels for 48% -> 44%
where the time goes in v2:
time: 79.2 us; the launch traced here: 79 us
  Pallas kernels  44.3 us (56%)
  starting transfers between devices  17.4 us (22%)
  waiting for transfers between devices  15.2 us (19%)
  local copies, waits for them, and re-layouts  1.96 us (2%)
    pallas_call x15, Pallas kernels, call(): pl.pallas_call(kernel, grid=grid, in_specs=list(in_specs) + [pl.BlockSpec...  31.9 us
    pallas_call x1, Pallas kernels, forward_own(): pl.pallas_call(own_kernel, in_specs=[pl.BlockSpec(memory_space=pltpu.VMEM...  9.96 us
    ppermute x8, starting transfers between devices, to_core(): return lax.ppermute(v, 'dp', [(i, i ^ 1) for i in range(4)])  6.85 us
    ppermute x8, waiting for transfers between devices, to_core(): return lax.ppermute(v, 'dp', [(i, i ^ 1) for i in range(4)])  4.73 us
    ppermute x1, starting transfers between devices, pipeline(): far_upper = lax.ppermute(upper, 'expert', [(2, 1), (1, 0)])  4.01 us
    ppermute x1, waiting for transfers between devices, pipeline(): far_lower = lax.ppermute(lower_out, 'expert', [(1, 2), (2, 3)])  3.81 us
    ppermute x4, waiting for transfers between devices, to_chip(): return lax.ppermute(v, 'dp', [(i, i ^ 2) for i in range(4)])  3.47 us
    ppermute x4, starting transfers between devices, to_chip(): return lax.ppermute(v, 'dp', [(i, i ^ 2) for i in range(4)])  3.12 us
  transfers between devices with their start and end apart: 16, of which 9 were waited for; matrix products, arithmetic and copies ran while one was open for 0% of the time, Pallas kernels for 44%

profile of v2, /device:TPU:21, one launch (start us, length us, event | category | flops | bytes accessed | tf_op | source)
XLA Modules:
  0.0 79.0 jit_solution(5420400754965484244)
XLA Ops:
  0.0 2.5 %pick.1.rows_ref.own_ref = bf16[2,48,1536]{2,1,0:T(8,128)(2,1)} custom-call(bf16[192,1536]{1,0:T(8,128)(2,1)} %refs_0_.1, bf16[192,1536]{1,0:T(8,128)(2,1)} %refs_1_.1, f32[4,192]{1,0:T(4,128)} %bitcast.3, s32[4,192]{1,0:T(4,128)} %bitcast.4, s32[1]{0:T(128)} %bitcast.2.refs_4_), custom_call_target="tpu_custom_call" | custom-call | flops 1000 | bytes 1000 | tf_op jit(solution)/shard_map/pick/pallas_call | solution.py:104
  2.5 1.3 %collective-permute-start.2 = (bf16[2,48,1536]{2,1,0:T(8,128)(2,1)}, bf16[2,48,1536]{2,1,0:T(8,128)(2,1)S(1)}, u32[]{:S(2)}, u32[]{:S(2)}) collective-permute-start(bf16[2,48,1536]{2,1,0:T(8,128)(2,1)} %pick.1.rows_ref.own_ref), channel_id=1, source_target_pairs={{0,4},{4,8},{8,12},{12,0},{1,5},{5,9},{9,13},{13,1},{2,6},{6,10},{... | collective-permute-start | bytes 884744 | tf_op jit(solution)/shard_map/ppermute | solution.py:313
  4.0 1.0 %copy-done = bf16[2,48,1536]{2,1,0:T(8,128)(2,1)S(1)} copy-done((bf16[2,48,1536]{2,1,0:T(8,128)(2,1)S(1)}, bf16[2,48,1536]{2,1,0:T(8,128)(2,1)}, u32[]{:S(2)}) %copy-start) | copy-done | bytes 294936
  5.0 10.0 %forward_own.1 = (f32[3,24,2688]{2,1,0:T(8,128)S(1)}, bf16[3,24,2688]{2,1,0:T(8,128)(2,1)S(1)}, bf16[3,2688,1536]{2,1,0:T(8,128)(2,1)S(1)}) custom-call(bf16[2,48,1536]{2,1,0:T(8,128)(2,1)S(1)} %copy-done, bf16[3,2688,1536]{2,1,0:T(8,128)(2,1)} %w_ref.1), custom_call_target="tpu_custom_call" | custom-call | flops 1000 | bytes 1000 | tf_op jit(solution)/shard_map/forward_own/pallas_call | solution.py:143
  15.0 1.3 %collective-permute-start = (bf16[3,24,2688]{2,1,0:T(8,128)(2,1)S(1)}, bf16[3,24,2688]{2,1,0:T(8,128)(2,1)S(1)}, u32[]{:S(2)}, u32[]{:S(2)}) collective-permute-start(bf16[3,24,2688]{2,1,0:T(8,128)(2,1)S(1)} %get-tuple-element.24), channel_id=1, source_target_pairs={{0,1},{1,0},{2,3},{3,2},{4,5},{5,4},{6,7},{7,6},{8,9},{9,8},{10,11... | collective-permute-start | bytes 1161224 | tf_op jit(solution)/shard_map/ppermute | solution.py:285
  16.3 0.6 collective-permute-done.3.upper_ref
  16.9 4.0 %collective-permute-start.5 = (bf16[2,48,1536]{2,1,0:T(8,128)(2,1)S(1)}, bf16[2,48,1536]{2,1,0:T(8,128)(2,1)S(1)}, u32[]{:S(2)}, u32[]{:S(2)}) collective-permute-start(bf16[2,48,1536]{2,1,0:T(8,128)(2,1)S(1)} %collective-permute-done.3.upper_ref), channel_id=1, source_target_pairs={{8,4},{4,0},{9,5},{5,1},{10,6},{6,2},{11,7},{7,3},{24,20},{20,16},... | collective-permute-start | bytes 884744 | tf_op jit(solution)/shard_map/ppermute | solution.py:318
  20.9 1.9 %collective-permute-start.4 = (bf16[2,48,1536]{2,1,0:T(8,128)(2,1)S(1)}, bf16[2,48,1536]{2,1,0:T(8,128)(2,1)S(1)}, u32[]{:S(2)}, u32[]{:S(2)}) collective-permute-start(bf16[2,48,1536]{2,1,0:T(8,128)(2,1)S(1)} %collective-permute-done.2.lower_ref), channel_id=1, source_target_pairs={{4,8},{8,12},{5,9},{9,13},{6,10},{10,14},{7,11},{11,15},{20,24},{2... | collective-permute-start | bytes 884744 | tf_op jit(solution)/shard_map/ppermute | solution.py:317
  23.0 1.3 %collective-permute-start.1 = (bf16[3,24,2688]{2,1,0:T(8,128)(2,1)S(1)}, bf16[3,24,2688]{2,1,0:T(8,128)(2,1)S(1)}, u32[]{:S(2)}, u32[]{:S(2)}) collective-permute-start(bf16[3,24,2688]{2,1,0:T(8,128)(2,1)S(1)} %get-tuple-element.26), channel_id=1, source_target_pairs={{0,2},{1,3},{2,0},{3,1},{4,6},{5,7},{6,4},{7,5},{8,10},{9,11},{10,... | collective-permute-start | bytes 1161224 | tf_op jit(solution)/shard_map/ppermute | solution.py:289
  24.3 2.5 %collective-permute-done.5.far_upper_ref = bf16[2,48,1536]{2,1,0:T(8,128)(2,1)S(1)} collective-permute-done((bf16[2,48,1536]{2,1,0:T(8,128)(2,1)S(1)}, bf16[2,48,1536]{2,1,0:T(8,128)(2,1)S(1)}, u32[]{:S(2)}, u32[]{:S(2)}) %collective-permute-start.5) | collective-permute-done | bytes 294944 | tf_op jit(solution)/shard_map/ppermute | solution.py:318
  26.8 3.8 %collective-permute-done.4.far_lower_ref = bf16[2,48,1536]{2,1,0:T(8,128)(2,1)S(1)} collective-permute-done((bf16[2,48,1536]{2,1,0:T(8,128)(2,1)S(1)}, bf16[2,48,1536]{2,1,0:T(8,128)(2,1)S(1)}, u32[]{:S(2)}, u32[]{:S(2)}) %collective-permute-start.4) | collective-permute-done | bytes 294944 | tf_op jit(solution)/shard_map/ppermute | solution.py:317
  30.6 1.0 %copy-done.1 = bf16[2,48,1536]{2,1,0:T(8,128)(2,1)S(1)} copy-done((bf16[2,48,1536]{2,1,0:T(8,128)(2,1)S(1)}, bf16[2,48,1536]{2,1,0:T(8,128)(2,1)}, u32[]{:S(2)}) %copy-start.1) | copy-done | bytes 294936
  31.6 2.7 %forward.3 = (f32[3,72,768]{2,1,0:T(8,128)S(1)}, bf16[3,72,768]{2,1,0:T(8,128)(2,1)S(1)}) custom-call(bf16[2,192,1536]{2,1,0:T(8,128)(2,1)S(1)} %arrange.1.rows_ref.refs_0_, bf16[3,2688,1536]{2,1,0:T(8,128)(2,1)S(1)} %get-tuple-element.28.w_ref, bf16[2,192,1536]{2,1,0:T(8,128)(2,1)S(1)} %arrange.1.rows_ref.refs_0_), custom_call_target="tpu_custom_call" | custom-call | flops 4000000000 | bytes 1000 | tf_op jit(solution)/shard_map/forward/pallas_call | solution.py:60
  34.3 1.7 %collective-permute-start.7 = (bf16[3,72,768]{2,1,0:T(8,128)(2,1)S(1)}, bf16[3,72,768]{2,1,0:T(8,128)(2,1)S(1)}, u32[]{:S(2)}, u32[]{:S(2)}) collective-permute-start(bf16[3,72,768]{2,1,0:T(8,128)(2,1)S(1)} %get-tuple-element.30), channel_id=1, source_target_pairs={{0,1},{1,0},{2,3},{3,2},{4,5},{5,4},{6,7},{7,6},{8,9},{9,8},{10,11... | collective-permute-start | bytes 995336 | tf_op jit(solution)/shard_map/ppermute | solution.py:285
  36.2 1.1 %collective-permute-done.7.received_ref = bf16[3,72,768]{2,1,0:T(8,128)(2,1)S(1)} collective-permute-done((bf16[3,72,768]{2,1,0:T(8,128)(2,1)S(1)}, bf16[3,72,768]{2,1,0:T(8,128)(2,1)S(1)}, u32[]{:S(2)}, u32[]{:S(2)}) %collective-permute-start.7) | collective-permute-done | bytes 331808 | tf_op jit(solution)/shard_map/ppermute | solution.py:285
  37.4 1.3 %collective-permute-start.9 = (bf16[3,72,768]{2,1,0:T(8,128)(2,1)S(1)}, bf16[3,72,768]{2,1,0:T(8,128)(2,1)S(1)}, u32[]{:S(2)}, u32[]{:S(2)}) collective-permute-start(bf16[3,72,768]{2,1,0:T(8,128)(2,1)S(1)} %get-tuple-element.35), channel_id=1, source_target_pairs={{0,2},{1,3},{2,0},{3,1},{4,6},{5,7},{6,4},{7,5},{8,10},{9,11},{10,... | collective-permute-start | bytes 995336 | tf_op jit(solution)/shard_map/ppermute | solution.py:289
  38.7 3.9 %forward.4 = (f32[3,72,1152]{2,1,0:T(8,128)S(1)}, bf16[3,72,1152]{2,1,0:T(8,128)(2,1)S(1)}) custom-call(bf16[2,192,1536]{2,1,0:T(8,128)(2,1)S(1)} %arrange.1.rows_ref.refs_0_, bf16[3,2688,1536]{2,1,0:T(8,128)(2,1)S(1)} %get-tuple-element.28.w_ref, f32[3,72,768]{2,1,0:T(8,128)S(1)} %get-tuple-element.31.refs_0_), custom_call_target="tpu_custom_call" | custom-call | flops 4000000000 | bytes 1000 | tf_op jit(solution)/shard_map/forward/pallas_call | solution.py:60
  42.6 0.7 collective-permute-start.10
  43.4 2.6 %forward.5 = (f32[3,72,768]{2,1,0:T(8,128)S(1)}, bf16[3,72,768]{2,1,0:T(8,128)(2,1)S(1)}) custom-call(bf16[2,192,1536]{2,1,0:T(8,128)(2,1)S(1)} %arrange.1.rows_ref.refs_0_, bf16[3,2688,1536]{2,1,0:T(8,128)(2,1)S(1)} %get-tuple-element.28.w_ref, f32[3,72,1152]{2,1,0:T(8,128)S(1)} %get-tuple-element.32.refs_0_.own_ref), custom_call_target="tpu_custom_call" | custom-call | flops 4000000000 | bytes 1000 | tf_op jit(solution)/shard_map/forward/pallas_call | solution.py:60
  46.2 0.3 collective-permute-start.12
  46.6 0.8 collective-permute-start.6
  47.5 0.4 collective-permute-start.13
  48.0 0.6 collective-permute-done.6.b_ref
  48.7 0.5 collective-permute-done.13.d_ref
  49.2 6.1 %backward.3.refs_2_.refs_0_ = f32[3,2688,1536]{2,1,0:T(8,128)} custom-call(bf16[3,24,2688]{2,1,0:T(8,128)(2,1)S(1)} %activate.4.refs_0_.a_ref, bf16[3,24,2688]{2,1,0:T(8,128)(2,1)S(1)} %collective-permute-done.6.b_ref, bf16[3,72,768]{2,1,0:T(8,128)(2,1)S(1)} %activate.5.refs_0_.c_ref, bf16[3,72,768]{2,1,0:T(8,128)(2,1)S(1)} %collective-permute-done.13.d_ref, ...), custom_call_target="tpu_custom_call" | custom-call | flops 1000 | bytes 1000 | tf_op jit(solution)/shard_map/backward/pallas_call | solution.py:60
  55.3 3.5 %collective-permute-done.12.refs_1_ = bf16[3,72,1152]{2,1,0:T(8,128)(2,1)S(1)} collective-permute-done((bf16[3,72,1152]{2,1,0:T(8,128)(2,1)S(1)}, bf16[3,72,1152]{2,1,0:T(8,128)(2,1)S(1)}, u32[]{:S(2)}, u32[]{:S(2)}) %collective-permute-start.12) | collective-permute-done | bytes 497696 | tf_op jit(solution)/shard_map/ppermute | solution.py:289
  59.0 1.4 %collective-permute-start.14 = (bf16[3,72,1152]{2,1,0:T(8,128)(2,1)S(1)}, bf16[3,72,1152]{2,1,0:T(8,128)(2,1)S(1)}, u32[]{:S(2)}, u32[]{:S(2)}) collective-permute-start(bf16[3,72,1152]{2,1,0:T(8,128)(2,1)S(1)} %activate.6.c_ref.refs_1_), channel_id=1, source_target_pairs={{0,1},{1,0},{2,3},{3,2},{4,5},{5,4},{6,7},{7,6},{8,9},{9,8},{10,11... | collective-permute-start | bytes 1493000 | tf_op jit(solution)/shard_map/ppermute | solution.py:285
  60.7 1.2 %collective-permute-done.14.d_ref = bf16[3,72,1152]{2,1,0:T(8,128)(2,1)S(1)} collective-permute-done((bf16[3,72,1152]{2,1,0:T(8,128)(2,1)S(1)}, bf16[3,72,1152]{2,1,0:T(8,128)(2,1)S(1)}, u32[]{:S(2)}, u32[]{:S(2)}) %collective-permute-start.14) | collective-permute-done | bytes 497696 | tf_op jit(solution)/shard_map/ppermute | solution.py:285
  61.9 8.7 %backward.4.refs_2_.refs_0_ = f32[3,2688,1536]{2,1,0:T(8,128)} custom-call(bf16[3,24,2688]{2,1,0:T(8,128)(2,1)S(1)} %activate.4.refs_0_.a_ref, bf16[3,24,2688]{2,1,0:T(8,128)(2,1)S(1)} %collective-permute-done.6.b_ref, bf16[3,72,1152]{2,1,0:T(8,128)(2,1)S(1)} %activate.6.c_ref.refs_1_, ...), custom_call_target="tpu_custom_call", output_to_operand_aliasing={{}: (5, {})} | custom-call | flops 1000 | bytes 1000 | tf_op jit(solution)/shard_map/backward/pallas_call | solution.py:60
  70.7 0.4 collective-permute-start.15
  71.2 1.3 %collective-permute-done.15.d_ref = bf16[3,72,768]{2,1,0:T(8,128)(2,1)S(1)} collective-permute-done((bf16[3,72,768]{2,1,0:T(8,128)(2,1)S(1)}, bf16[3,72,768]{2,1,0:T(8,128)(2,1)S(1)}, u32[]{:S(2)}, u32[]{:S(2)}) %collective-permute-start.15) | collective-permute-done | bytes 331808 | tf_op jit(solution)/shard_map/ppermute | solution.py:285
  72.4 6.5 %backward.5 = f32[3,2688,1536]{2,1,0:T(8,128)} custom-call(bf16[3,24,2688]{2,1,0:T(8,128)(2,1)S(1)} %activate.4.refs_0_.a_ref, bf16[3,24,2688]{2,1,0:T(8,128)(2,1)S(1)} %collective-permute-done.6.b_ref, bf16[3,72,768]{2,1,0:T(8,128)(2,1)S(1)} %activate.7.c_ref.refs_1_, ...), custom_call_target="tpu_custom_call", output_to_operand_aliasing={{}: (5, {})} | custom-call | flops 1000 | bytes 1000 | tf_op jit(solution)/shard_map/backward/pallas_call | solution.py:60
  (21 shorter events, 1.9 us)
Async XLA Ops:
  2.5 13.8 %collective-permute-start.2 = (bf16[2,48,1536]{2,1,0:T(8,128)(2,1)}, bf16[2,48,1536]{2,1,0:T(8,128)(2,1)S(1)}, u32[]{:S(2)}, u32[]{:S(2)}) collective-permute-start(bf16[2,48,1536]{2,1,0:T(8,128)(2,1)} %pick.1.rows_ref.own_ref), channel_id=1, source_target_pairs={{0,4},{4,8},{8,12},{12,0},{1,5},{5,9},{9,13},{13,1},{2,6},{6,10},{... | collective-permute-start | bytes 884744 | tf_op jit(solution)/shard_map/ppermute | solution.py:313
  3.8 13.1 %collective-permute-start.3 = (bf16[2,48,1536]{2,1,0:T(8,128)(2,1)}, bf16[2,48,1536]{2,1,0:T(8,128)(2,1)S(1)}, u32[]{:S(2)}, u32[]{:S(2)}) collective-permute-start(bf16[2,48,1536]{2,1,0:T(8,128)(2,1)} %pick.1.rows_ref.own_ref), channel_id=1, source_target_pairs={{0,12},{4,0},{8,4},{12,8},{1,13},{5,1},{9,5},{13,9},{2,14},{6,2},{... | collective-permute-start | bytes 884744 | tf_op jit(solution)/shard_map/ppermute | solution.py:314
  4.0 1.0 %copy-start = (bf16[2,48,1536]{2,1,0:T(8,128)(2,1)S(1)}, bf16[2,48,1536]{2,1,0:T(8,128)(2,1)}, u32[]{:S(2)}) copy-start(bf16[2,48,1536]{2,1,0:T(8,128)(2,1)} %pick.1.rows_ref.own_ref) | copy-start | bytes 884740
  15.0 7.9 %collective-permute-start = (bf16[3,24,2688]{2,1,0:T(8,128)(2,1)S(1)}, bf16[3,24,2688]{2,1,0:T(8,128)(2,1)S(1)}, u32[]{:S(2)}, u32[]{:S(2)}) collective-permute-start(bf16[3,24,2688]{2,1,0:T(8,128)(2,1)S(1)} %get-tuple-element.24), channel_id=1, source_target_pairs={{0,1},{1,0},{2,3},{3,2},{4,5},{5,4},{6,7},{7,6},{8,9},{9,8},{10,11... | collective-permute-start | bytes 1161224 | tf_op jit(solution)/shard_map/ppermute | solution.py:285
  16.9 9.9 %collective-permute-start.5 = (bf16[2,48,1536]{2,1,0:T(8,128)(2,1)S(1)}, bf16[2,48,1536]{2,1,0:T(8,128)(2,1)S(1)}, u32[]{:S(2)}, u32[]{:S(2)}) collective-permute-start(bf16[2,48,1536]{2,1,0:T(8,128)(2,1)S(1)} %collective-permute-done.3.upper_ref), channel_id=1, source_target_pairs={{8,4},{4,0},{9,5},{5,1},{10,6},{6,2},{11,7},{7,3},{24,20},{20,16},... | collective-permute-start | bytes 884744 | tf_op jit(solution)/shard_map/ppermute | solution.py:318
  20.9 9.7 %collective-permute-start.4 = (bf16[2,48,1536]{2,1,0:T(8,128)(2,1)S(1)}, bf16[2,48,1536]{2,1,0:T(8,128)(2,1)S(1)}, u32[]{:S(2)}, u32[]{:S(2)}) collective-permute-start(bf16[2,48,1536]{2,1,0:T(8,128)(2,1)S(1)} %collective-permute-done.2.lower_ref), channel_id=1, source_target_pairs={{4,8},{8,12},{5,9},{9,13},{6,10},{10,14},{7,11},{11,15},{20,24},{2... | collective-permute-start | bytes 884744 | tf_op jit(solution)/shard_map/ppermute | solution.py:317
  23.0 13.1 %collective-permute-start.1 = (bf16[3,24,2688]{2,1,0:T(8,128)(2,1)S(1)}, bf16[3,24,2688]{2,1,0:T(8,128)(2,1)S(1)}, u32[]{:S(2)}, u32[]{:S(2)}) collective-permute-start(bf16[3,24,2688]{2,1,0:T(8,128)(2,1)S(1)} %get-tuple-element.26), channel_id=1, source_target_pairs={{0,2},{1,3},{2,0},{3,1},{4,6},{5,7},{6,4},{7,5},{8,10},{9,11},{10,... | collective-permute-start | bytes 1161224 | tf_op jit(solution)/shard_map/ppermute | solution.py:289
  30.6 1.0 %copy-start.1 = (bf16[2,48,1536]{2,1,0:T(8,128)(2,1)S(1)}, bf16[2,48,1536]{2,1,0:T(8,128)(2,1)}, u32[]{:S(2)}) copy-start(bf16[2,48,1536]{2,1,0:T(8,128)(2,1)} %pick.1.rows_ref.own_ref) | copy-start | bytes 884740
  34.3 3.0 %collective-permute-start.7 = (bf16[3,72,768]{2,1,0:T(8,128)(2,1)S(1)}, bf16[3,72,768]{2,1,0:T(8,128)(2,1)S(1)}, u32[]{:S(2)}, u32[]{:S(2)}) collective-permute-start(bf16[3,72,768]{2,1,0:T(8,128)(2,1)S(1)} %get-tuple-element.30), channel_id=1, source_target_pairs={{0,1},{1,0},{2,3},{3,2},{4,5},{5,4},{6,7},{7,6},{8,9},{9,8},{10,11... | collective-permute-start | bytes 995336 | tf_op jit(solution)/shard_map/ppermute | solution.py:285
  37.4 9.9 %collective-permute-start.9 = (bf16[3,72,768]{2,1,0:T(8,128)(2,1)S(1)}, bf16[3,72,768]{2,1,0:T(8,128)(2,1)S(1)}, u32[]{:S(2)}, u32[]{:S(2)}) collective-permute-start(bf16[3,72,768]{2,1,0:T(8,128)(2,1)S(1)} %get-tuple-element.35), channel_id=1, source_target_pairs={{0,2},{1,3},{2,0},{3,1},{4,6},{5,7},{6,4},{7,5},{8,10},{9,11},{10,... | collective-permute-start | bytes 995336 | tf_op jit(solution)/shard_map/ppermute | solution.py:289
  42.6 3.5 %collective-permute-start.10 = (bf16[3,72,1152]{2,1,0:T(8,128)(2,1)S(1)}, bf16[3,72,1152]{2,1,0:T(8,128)(2,1)S(1)}, u32[]{:S(2)}, u32[]{:S(2)}) collective-permute-start(bf16[3,72,1152]{2,1,0:T(8,128)(2,1)S(1)} %get-tuple-element.36), channel_id=1, source_target_pairs={{0,1},{1,0},{2,3},{3,2},{4,5},{5,4},{6,7},{7,6},{8,9},{9,8},{10,11... | collective-permute-start | bytes 1493000 | tf_op jit(solution)/shard_map/ppermute | solution.py:285
  46.0 1.9 %collective-permute-start.8 = (bf16[3,72,768]{2,1,0:T(8,128)(2,1)S(1)}, bf16[3,72,768]{2,1,0:T(8,128)(2,1)S(1)}, u32[]{:S(2)}, u32[]{:S(2)}) collective-permute-start(bf16[3,72,768]{2,1,0:T(8,128)(2,1)S(1)} %get-tuple-element.34), channel_id=1, source_target_pairs={{0,1},{1,0},{2,3},{3,2},{4,5},{5,4},{6,7},{7,6},{8,9},{9,8},{10,11... | collective-permute-start | bytes 995336 | tf_op jit(solution)/shard_map/ppermute | solution.py:285
  46.2 12.5 %collective-permute-start.12 = (bf16[3,72,1152]{2,1,0:T(8,128)(2,1)S(1)}, bf16[3,72,1152]{2,1,0:T(8,128)(2,1)S(1)}, u32[]{:S(2)}, u32[]{:S(2)}) collective-permute-start(bf16[3,72,1152]{2,1,0:T(8,128)(2,1)S(1)} %get-tuple-element.40), channel_id=1, source_target_pairs={{0,2},{1,3},{2,0},{3,1},{4,6},{5,7},{6,4},{7,5},{8,10},{9,11},{10,... | collective-permute-start | bytes 1493000 | tf_op jit(solution)/shard_map/ppermute | solution.py:289
  46.6 2.1 %collective-permute-start.6 = (bf16[3,24,2688]{2,1,0:T(8,128)(2,1)S(1)}, bf16[3,24,2688]{2,1,0:T(8,128)(2,1)S(1)}, u32[]{:S(2)}, u32[]{:S(2)}) collective-permute-start(bf16[3,24,2688]{2,1,0:T(8,128)(2,1)S(1)} %activate.4.refs_0_.a_ref), channel_id=1, source_target_pairs={{0,1},{1,0},{2,3},{3,2},{4,5},{5,4},{6,7},{7,6},{8,9},{9,8},{10,11... | collective-permute-start | bytes 1161224 | tf_op jit(solution)/shard_map/ppermute | solution.py:285
  47.5 1.7 %collective-permute-start.13 = (bf16[3,72,768]{2,1,0:T(8,128)(2,1)S(1)}, bf16[3,72,768]{2,1,0:T(8,128)(2,1)S(1)}, u32[]{:S(2)}, u32[]{:S(2)}) collective-permute-start(bf16[3,72,768]{2,1,0:T(8,128)(2,1)S(1)} %activate.5.refs_0_.c_ref), channel_id=1, source_target_pairs={{0,1},{1,0},{2,3},{3,2},{4,5},{5,4},{6,7},{7,6},{8,9},{9,8},{10,11... | collective-permute-start | bytes 995336 | tf_op jit(solution)/shard_map/ppermute | solution.py:285
  59.0 2.9 %collective-permute-start.14 = (bf16[3,72,1152]{2,1,0:T(8,128)(2,1)S(1)}, bf16[3,72,1152]{2,1,0:T(8,128)(2,1)S(1)}, u32[]{:S(2)}, u32[]{:S(2)}) collective-permute-start(bf16[3,72,1152]{2,1,0:T(8,128)(2,1)S(1)} %activate.6.c_ref.refs_1_), channel_id=1, source_target_pairs={{0,1},{1,0},{2,3},{3,2},{4,5},{5,4},{6,7},{7,6},{8,9},{9,8},{10,11... | collective-permute-start | bytes 1493000 | tf_op jit(solution)/shard_map/ppermute | solution.py:285
  60.4 10.2 %collective-permute-start.11 = (bf16[3,72,768]{2,1,0:T(8,128)(2,1)S(1)}, bf16[3,72,768]{2,1,0:T(8,128)(2,1)S(1)}, u32[]{:S(2)}, u32[]{:S(2)}) collective-permute-start(bf16[3,72,768]{2,1,0:T(8,128)(2,1)S(1)} %get-tuple-element.39), channel_id=1, source_target_pairs={{0,2},{1,3},{2,0},{3,1},{4,6},{5,7},{6,4},{7,5},{8,10},{9,11},{10,... | collective-permute-start | bytes 995336 | tf_op jit(solution)/shard_map/ppermute | solution.py:289
  70.7 1.7 %collective-permute-start.15 = (bf16[3,72,768]{2,1,0:T(8,128)(2,1)S(1)}, bf16[3,72,768]{2,1,0:T(8,128)(2,1)S(1)}, u32[]{:S(2)}, u32[]{:S(2)}) collective-permute-start(bf16[3,72,768]{2,1,0:T(8,128)(2,1)S(1)} %activate.7.c_ref.refs_1_), channel_id=1, source_target_pairs={{0,1},{1,0},{2,3},{3,2},{4,5},{5,4},{6,7},{7,6},{8,9},{9,8},{10,11... | collective-permute-start | bytes 995336 | tf_op jit(solution)/shard_map/ppermute | solution.py:285

commit v3 on v2

--- a/solution.py
+++ b/solution.py
@@ -8,10 +8,11 @@
 from jax.sharding import PartitionSpec as P
 
 STEP = 384
-BACK_BLOCKS = (256, 384)
-REST_CHUNKS = (2, 3, 2)
-AHEAD = (1, 2, 3)
+BACK_BLOCKS = (256, 128)
+REST_CHUNKS = (2, 2, 2, 1)
+AHEAD = (1, 2, 4, 4)
 DEFER = 1
+FENCES = (0, 1, 2)
 VMEM = 24 * 1024 * 1024
 SMALL = 8 * 1024 * 1024
 LARGE = 253 * 256 * 1024
@@ -281,6 +282,16 @@
     return call(arrange_kernel, "arrange", blocks, [whole] * 5, whole, shape, after)
 
 
+def fence_kernel(*refs):
+    refs[-1][...] = jnp.zeros(refs[-1].shape, jnp.float32)
+
+
+def fence(after):
+    whole = pl.BlockSpec(memory_space=pltpu.VMEM)
+    shape = jax.ShapeDtypeStruct((8, 128), jnp.float32)
+    return call(fence_kernel, "fence", (), [], whole, shape, after, flops=FINAL_FLOPS)
+
+
 def to_core(v):
     return lax.ppermute(v, "dp", [(i, i ^ 1) for i in range(4)])
 
@@ -334,6 +345,8 @@
                 total, sent = add(*final, last, FINAL_FLOPS)
                 sums.append((total, to_chip(sent)))
                 last = (total,)
+        if k in FENCES:
+            last = (fence(last),)
         after = () if grads is not None and last[0] is grads else last
         grads = backward(
             own_left + lefts[k], rows, grads, weights.shape, firsts[k], REST_CHUNKS[k], after

time: 79.2 us -> 78.1 us (0.986)
  waiting for transfers between devices: 15.2 us -> 10.5 us
  starting transfers between devices: 17.4 us -> 20.1 us
  Pallas kernels: 44.3 us -> 45.2 us
    ppermute x4 -> x5, waiting for transfers between devices: 3.47 us -> 0.29 us  [to_chip(): return lax.ppermute(v, 'dp', [(i, i ^ 2) for i in range(4)])]
    ppermute x8 -> x10, waiting for transfers between devices: 4.73 us -> 3.21 us  [to_core(): return lax.ppermute(v, 'dp', [(i, i ^ 1) for i in range(4)])]
    ppermute x8 -> x10, starting transfers between devices: 6.85 us -> 8.22 us  [to_core(): return lax.ppermute(v, 'dp', [(i, i ^ 1) for i in range(4)])]
    ppermute x4 -> x5, starting transfers between devices: 3.12 us -> 4.41 us  [to_chip(): return lax.ppermute(v, 'dp', [(i, i ^ 2) for i in range(4)])]
    pallas_call x15 -> x22, Pallas kernels: 31.9 us -> 32.8 us  [call(): pl.pallas_call(kernel, grid=grid, in_specs=list(in_specs) + [pl.BlockSpec...]
  transfers between devices with their start and end apart: 16 -> 19, of which waited for: 9 -> 7; matrix products, arithmetic and copies ran while one was open for 0% -> 0% of each run, Pallas kernels for 44% -> 50%
where the time goes in v3:
time: 78.1 us; the launch traced here: 77.8 us
  Pallas kernels  45.2 us (58%)
  starting transfers between devices  20.1 us (26%)
  waiting for transfers between devices  10.5 us (13%)
  local copies, waits for them, and re-layouts  1.96 us (3%)
    pallas_call x22, Pallas kernels, call(): pl.pallas_call(kernel, grid=grid, in_specs=list(in_specs) + [pl.BlockSpec...  32.8 us
    pallas_call x1, Pallas kernels, forward_own(): pl.pallas_call(own_kernel, in_specs=[pl.BlockSpec(memory_space=pltpu.VMEM...  9.96 us
    ppermute x10, starting transfers between devices, to_core(): return lax.ppermute(v, 'dp', [(i, i ^ 1) for i in range(4)])  8.22 us
    ppermute x5, starting transfers between devices, to_chip(): return lax.ppermute(v, 'dp', [(i, i ^ 2) for i in range(4)])  4.41 us
    ppermute x1, starting transfers between devices, pipeline(): far_upper = lax.ppermute(upper, 'expert', [(2, 1), (1, 0)])  4.01 us
    ppermute x1, waiting for transfers between devices, pipeline(): far_lower = lax.ppermute(lower_out, 'expert', [(1, 2), (2, 3)])  3.81 us
    ppermute x10, waiting for transfers between devices, to_core(): return lax.ppermute(v, 'dp', [(i, i ^ 1) for i in range(4)])  3.21 us
    ppermute x1, waiting for transfers between devices, pipeline(): far_upper = lax.ppermute(upper, 'expert', [(2, 1), (1, 0)])  2.51 us
  transfers between devices with their start and end apart: 19, of which 7 were waited for; matrix products, arithmetic and copies ran while one was open for 0% of the time, Pallas kernels for 50%

profile of v3, /device:TPU:21, one launch (start us, length us, event | category | flops | bytes accessed | tf_op | source)
XLA Modules:
  0.0 77.8 jit_solution(6929937606796294384)
XLA Ops:
  0.0 2.5 %pick.1.rows_ref.own_ref = bf16[2,48,1536]{2,1,0:T(8,128)(2,1)} custom-call(bf16[192,1536]{1,0:T(8,128)(2,1)} %refs_0_.1, bf16[192,1536]{1,0:T(8,128)(2,1)} %refs_1_.1, f32[4,192]{1,0:T(4,128)} %bitcast.3, s32[4,192]{1,0:T(4,128)} %bitcast.4, s32[1]{0:T(128)} %bitcast.2.refs_4_), custom_call_target="tpu_custom_call" | custom-call | flops 1000 | bytes 1000 | tf_op jit(solution)/shard_map/pick/pallas_call | solution.py:105
  2.5 1.3 %collective-permute-start.2 = (bf16[2,48,1536]{2,1,0:T(8,128)(2,1)}, bf16[2,48,1536]{2,1,0:T(8,128)(2,1)S(1)}, u32[]{:S(2)}, u32[]{:S(2)}) collective-permute-start(bf16[2,48,1536]{2,1,0:T(8,128)(2,1)} %pick.1.rows_ref.own_ref), channel_id=1, source_target_pairs={{0,4},{4,8},{8,12},{12,0},{1,5},{5,9},{9,13},{13,1},{2,6},{6,10},{... | collective-permute-start | bytes 884744 | tf_op jit(solution)/shard_map/ppermute | solution.py:324
  4.0 1.0 %copy-done = bf16[2,48,1536]{2,1,0:T(8,128)(2,1)S(1)} copy-done((bf16[2,48,1536]{2,1,0:T(8,128)(2,1)S(1)}, bf16[2,48,1536]{2,1,0:T(8,128)(2,1)}, u32[]{:S(2)}) %copy-start) | copy-done | bytes 294936
  5.0 10.0 %forward_own.1 = (f32[3,24,2688]{2,1,0:T(8,128)S(1)}, bf16[3,24,2688]{2,1,0:T(8,128)(2,1)S(1)}, bf16[3,2688,1536]{2,1,0:T(8,128)(2,1)S(1)}) custom-call(bf16[2,48,1536]{2,1,0:T(8,128)(2,1)S(1)} %copy-done, bf16[3,2688,1536]{2,1,0:T(8,128)(2,1)} %w_ref.1), custom_call_target="tpu_custom_call" | custom-call | flops 1000 | bytes 1000 | tf_op jit(solution)/shard_map/forward_own/pallas_call | solution.py:144
  15.0 1.3 %collective-permute-start = (bf16[3,24,2688]{2,1,0:T(8,128)(2,1)S(1)}, bf16[3,24,2688]{2,1,0:T(8,128)(2,1)S(1)}, u32[]{:S(2)}, u32[]{:S(2)}) collective-permute-start(bf16[3,24,2688]{2,1,0:T(8,128)(2,1)S(1)} %get-tuple-element.28), channel_id=1, source_target_pairs={{0,1},{1,0},{2,3},{3,2},{4,5},{5,4},{6,7},{7,6},{8,9},{9,8},{10,11... | collective-permute-start | bytes 1161224 | tf_op jit(solution)/shard_map/ppermute | solution.py:296
  16.3 0.6 collective-permute-done.3.upper_ref
  16.9 4.0 %collective-permute-start.5 = (bf16[2,48,1536]{2,1,0:T(8,128)(2,1)S(1)}, bf16[2,48,1536]{2,1,0:T(8,128)(2,1)S(1)}, u32[]{:S(2)}, u32[]{:S(2)}) collective-permute-start(bf16[2,48,1536]{2,1,0:T(8,128)(2,1)S(1)} %collective-permute-done.3.upper_ref), channel_id=1, source_target_pairs={{8,4},{4,0},{9,5},{5,1},{10,6},{6,2},{11,7},{7,3},{24,20},{20,16},... | collective-permute-start | bytes 884744 | tf_op jit(solution)/shard_map/ppermute | solution.py:329
  20.9 1.9 %collective-permute-start.4 = (bf16[2,48,1536]{2,1,0:T(8,128)(2,1)S(1)}, bf16[2,48,1536]{2,1,0:T(8,128)(2,1)S(1)}, u32[]{:S(2)}, u32[]{:S(2)}) collective-permute-start(bf16[2,48,1536]{2,1,0:T(8,128)(2,1)S(1)} %collective-permute-done.2.lower_ref), channel_id=1, source_target_pairs={{4,8},{8,12},{5,9},{9,13},{6,10},{10,14},{7,11},{11,15},{20,24},{2... | collective-permute-start | bytes 884744 | tf_op jit(solution)/shard_map/ppermute | solution.py:328
  23.0 1.3 %collective-permute-start.1 = (bf16[3,24,2688]{2,1,0:T(8,128)(2,1)S(1)}, bf16[3,24,2688]{2,1,0:T(8,128)(2,1)S(1)}, u32[]{:S(2)}, u32[]{:S(2)}) collective-permute-start(bf16[3,24,2688]{2,1,0:T(8,128)(2,1)S(1)} %get-tuple-element.30), channel_id=1, source_target_pairs={{0,2},{1,3},{2,0},{3,1},{4,6},{5,7},{6,4},{7,5},{8,10},{9,11},{10,... | collective-permute-start | bytes 1161224 | tf_op jit(solution)/shard_map/ppermute | solution.py:300
  24.3 2.5 %collective-permute-done.5.far_upper_ref = bf16[2,48,1536]{2,1,0:T(8,128)(2,1)S(1)} collective-permute-done((bf16[2,48,1536]{2,1,0:T(8,128)(2,1)S(1)}, bf16[2,48,1536]{2,1,0:T(8,128)(2,1)S(1)}, u32[]{:S(2)}, u32[]{:S(2)}) %collective-permute-start.5) | collective-permute-done | bytes 294944 | tf_op jit(solution)/shard_map/ppermute | solution.py:329
  26.8 3.8 %collective-permute-done.4.far_lower_ref = bf16[2,48,1536]{2,1,0:T(8,128)(2,1)S(1)} collective-permute-done((bf16[2,48,1536]{2,1,0:T(8,128)(2,1)S(1)}, bf16[2,48,1536]{2,1,0:T(8,128)(2,1)S(1)}, u32[]{:S(2)}, u32[]{:S(2)}) %collective-permute-start.4) | collective-permute-done | bytes 294944 | tf_op jit(solution)/shard_map/ppermute | solution.py:328
  30.6 1.0 %copy-done.1 = bf16[2,48,1536]{2,1,0:T(8,128)(2,1)S(1)} copy-done((bf16[2,48,1536]{2,1,0:T(8,128)(2,1)S(1)}, bf16[2,48,1536]{2,1,0:T(8,128)(2,1)}, u32[]{:S(2)}) %copy-start.1) | copy-done | bytes 294936
  31.7 2.6 %forward.4 = (f32[3,72,768]{2,1,0:T(8,128)S(1)}, bf16[3,72,768]{2,1,0:T(8,128)(2,1)S(1)}) custom-call(bf16[2,192,1536]{2,1,0:T(8,128)(2,1)S(1)} %arrange.1.rows_ref.refs_0_, bf16[3,2688,1536]{2,1,0:T(8,128)(2,1)S(1)} %get-tuple-element.32.w_ref, bf16[2,192,1536]{2,1,0:T(8,128)(2,1)S(1)} %arrange.1.rows_ref.refs_0_), custom_call_target="tpu_custom_call" | custom-call | flops 4000000000 | bytes 1000 | tf_op jit(solution)/shard_map/forward/pallas_call | solution.py:61
  34.3 1.7 %collective-permute-start.7 = (bf16[3,72,768]{2,1,0:T(8,128)(2,1)S(1)}, bf16[3,72,768]{2,1,0:T(8,128)(2,1)S(1)}, u32[]{:S(2)}, u32[]{:S(2)}) collective-permute-start(bf16[3,72,768]{2,1,0:T(8,128)(2,1)S(1)} %get-tuple-element.34), channel_id=1, source_target_pairs={{0,1},{1,0},{2,3},{3,2},{4,5},{5,4},{6,7},{7,6},{8,9},{9,8},{10,11... | collective-permute-start | bytes 995336 | tf_op jit(solution)/shard_map/ppermute | solution.py:296
  36.2 1.1 %collective-permute-done.7.received_ref = bf16[3,72,768]{2,1,0:T(8,128)(2,1)S(1)} collective-permute-done((bf16[3,72,768]{2,1,0:T(8,128)(2,1)S(1)}, bf16[3,72,768]{2,1,0:T(8,128)(2,1)S(1)}, u32[]{:S(2)}, u32[]{:S(2)}) %collective-permute-start.7) | collective-permute-done | bytes 331808 | tf_op jit(solution)/shard_map/ppermute | solution.py:296
  37.4 1.3 %collective-permute-start.10 = (bf16[3,72,768]{2,1,0:T(8,128)(2,1)S(1)}, bf16[3,72,768]{2,1,0:T(8,128)(2,1)S(1)}, u32[]{:S(2)}, u32[]{:S(2)}) collective-permute-start(bf16[3,72,768]{2,1,0:T(8,128)(2,1)S(1)} %get-tuple-element.42), channel_id=1, source_target_pairs={{0,2},{1,3},{2,0},{3,1},{4,6},{5,7},{6,4},{7,5},{8,10},{9,11},{10,... | collective-permute-start | bytes 995336 | tf_op jit(solution)/shard_map/ppermute | solution.py:300
  38.7 2.6 %forward.5 = (f32[3,72,768]{2,1,0:T(8,128)S(1)}, bf16[3,72,768]{2,1,0:T(8,128)(2,1)S(1)}) custom-call(bf16[2,192,1536]{2,1,0:T(8,128)(2,1)S(1)} %arrange.1.rows_ref.refs_0_, bf16[3,2688,1536]{2,1,0:T(8,128)(2,1)S(1)} %get-tuple-element.32.w_ref, f32[3,72,768]{2,1,0:T(8,128)S(1)} %get-tuple-element.35.refs_0_), custom_call_target="tpu_custom_call" | custom-call | flops 4000000000 | bytes 1000 | tf_op jit(solution)/shard_map/forward/pallas_call | solution.py:61
  41.3 0.7 collective-permute-start.8
  42.0 2.6 %forward.6 = (f32[3,72,768]{2,1,0:T(8,128)S(1)}, bf16[3,72,768]{2,1,0:T(8,128)(2,1)S(1)}) custom-call(bf16[2,192,1536]{2,1,0:T(8,128)(2,1)S(1)} %arrange.1.rows_ref.refs_0_, bf16[3,2688,1536]{2,1,0:T(8,128)(2,1)S(1)} %get-tuple-element.32.w_ref, f32[3,72,768]{2,1,0:T(8,128)S(1)} %get-tuple-element.36.refs_0_.own_ref), custom_call_target="tpu_custom_call" | custom-call | flops 4000000000 | bytes 1000 | tf_op jit(solution)/shard_map/forward/pallas_call | solution.py:61
  44.9 1.3 %forward.7 = (f32[3,72,384]{2,1,0:T(8,128)S(1)}, bf16[3,72,384]{2,1,0:T(8,128)(2,1)S(1)}) custom-call(bf16[2,192,1536]{2,1,0:T(8,128)(2,1)S(1)} %arrange.1.rows_ref.refs_0_, bf16[3,2688,1536]{2,1,0:T(8,128)(2,1)S(1)} %get-tuple-element.32.w_ref, f32[3,72,768]{2,1,0:T(8,128)S(1)} %get-tuple-element.39.refs_0_), custom_call_target="tpu_custom_call" | custom-call | flops 4000000000 | bytes 1000 | tf_op jit(solution)/shard_map/forward/pallas_call | solution.py:61
  46.1 0.5 collective-permute-start.9
  47.1 1.3 %collective-permute-start.13 = (bf16[3,72,768]{2,1,0:T(8,128)(2,1)S(1)}, bf16[3,72,768]{2,1,0:T(8,128)(2,1)S(1)}, u32[]{:S(2)}, u32[]{:S(2)}) collective-permute-start(bf16[3,72,768]{2,1,0:T(8,128)(2,1)S(1)} %get-tuple-element.47), channel_id=1, source_target_pairs={{0,2},{1,3},{2,0},{3,1},{4,6},{5,7},{6,4},{7,5},{8,10},{9,11},{10,... | collective-permute-start | bytes 995336 | tf_op jit(solution)/shard_map/ppermute | solution.py:300
  48.6 1.1 %collective-permute-start.15 = (bf16[3,72,768]{2,1,0:T(8,128)(2,1)S(1)}, bf16[3,72,768]{2,1,0:T(8,128)(2,1)S(1)}, u32[]{:S(2)}, u32[]{:S(2)}) collective-permute-start(bf16[3,72,768]{2,1,0:T(8,128)(2,1)S(1)} %activate.6.refs_0_.c_ref), channel_id=1, source_target_pairs={{0,1},{1,0},{2,3},{3,2},{4,5},{5,4},{6,7},{7,6},{8,9},{9,8},{10,11... | collective-permute-start | bytes 995336 | tf_op jit(solution)/shard_map/ppermute | solution.py:296
  50.0 0.9 %collective-permute-done.15.d_ref = bf16[3,72,768]{2,1,0:T(8,128)(2,1)S(1)} collective-permute-done((bf16[3,72,768]{2,1,0:T(8,128)(2,1)S(1)}, bf16[3,72,768]{2,1,0:T(8,128)(2,1)S(1)}, u32[]{:S(2)}, u32[]{:S(2)}) %collective-permute-start.15) | collective-permute-done | bytes 331808 | tf_op jit(solution)/shard_map/ppermute | solution.py:296
  50.9 6.1 %backward.4.refs_2_.refs_0_ = f32[3,2688,1536]{2,1,0:T(8,128)} custom-call(bf16[3,24,2688]{2,1,0:T(8,128)(2,1)S(1)} %activate.5.refs_0_.a_ref, bf16[3,24,2688]{2,1,0:T(8,128)(2,1)S(1)} %collective-permute-done.6.b_ref, bf16[3,72,768]{2,1,0:T(8,128)(2,1)S(1)} %activate.6.refs_0_.c_ref, bf16[3,72,768]{2,1,0:T(8,128)(2,1)S(1)} %collective-permute-done.15.d_ref, ...), custom_call_target="tpu_custom_call" | custom-call | flops 1000 | bytes 1000 | tf_op jit(solution)/shard_map/backward/pallas_call | solution.py:61
  57.2 0.9 %collective-permute-start.16 = (bf16[3,72,768]{2,1,0:T(8,128)(2,1)S(1)}, bf16[3,72,768]{2,1,0:T(8,128)(2,1)S(1)}, u32[]{:S(2)}, u32[]{:S(2)}) collective-permute-start(bf16[3,72,768]{2,1,0:T(8,128)(2,1)S(1)} %activate.7.refs_0_.c_ref), channel_id=1, source_target_pairs={{0,1},{1,0},{2,3},{3,2},{4,5},{5,4},{6,7},{7,6},{8,9},{9,8},{10,11... | collective-permute-start | bytes 995336 | tf_op jit(solution)/shard_map/ppermute | solution.py:296
  58.1 1.3 %collective-permute-done.16.d_ref = bf16[3,72,768]{2,1,0:T(8,128)(2,1)S(1)} collective-permute-done((bf16[3,72,768]{2,1,0:T(8,128)(2,1)S(1)}, bf16[3,72,768]{2,1,0:T(8,128)(2,1)S(1)}, u32[]{:S(2)}, u32[]{:S(2)}) %collective-permute-start.16) | collective-permute-done | bytes 331808 | tf_op jit(solution)/shard_map/ppermute | solution.py:296
  59.3 6.1 %backward.5.refs_2_.refs_0_ = f32[3,2688,1536]{2,1,0:T(8,128)} custom-call(bf16[3,24,2688]{2,1,0:T(8,128)(2,1)S(1)} %activate.5.refs_0_.a_ref, bf16[3,24,2688]{2,1,0:T(8,128)(2,1)S(1)} %collective-permute-done.6.b_ref, bf16[3,72,768]{2,1,0:T(8,128)(2,1)S(1)} %activate.7.refs_0_.c_ref, ...), custom_call_target="tpu_custom_call", output_to_operand_aliasing={{}: (5, {})} | custom-call | flops 1000 | bytes 1000 | tf_op jit(solution)/shard_map/backward/pallas_call | solution.py:61
  65.6 0.4 collective-permute-start.18
  66.4 1.3 %collective-permute-start.17 = (bf16[3,72,384]{2,1,0:T(8,128)(2,1)S(1)}, bf16[3,72,384]{2,1,0:T(8,128)(2,1)S(1)}, u32[]{:S(2)}, u32[]{:S(2)}) collective-permute-start(bf16[3,72,384]{2,1,0:T(8,128)(2,1)S(1)} %activate.9.refs_0_.c_ref), channel_id=1, source_target_pairs={{0,1},{1,0},{2,3},{3,2},{4,5},{5,4},{6,7},{7,6},{8,9},{9,8},{10,11... | collective-permute-start | bytes 497672 | tf_op jit(solution)/shard_map/ppermute | solution.py:296
  67.8 6.2 %backward.6.refs_0_ = f32[3,2688,1536]{2,1,0:T(8,128)} custom-call(bf16[3,24,2688]{2,1,0:T(8,128)(2,1)S(1)} %activate.5.refs_0_.a_ref, bf16[3,24,2688]{2,1,0:T(8,128)(2,1)S(1)} %collective-permute-done.6.b_ref, bf16[3,72,768]{2,1,0:T(8,128)(2,1)S(1)} %activate.8.refs_2_.c_ref, ...), custom_call_target="tpu_custom_call", output_to_operand_aliasing={{}: (5, {})} | custom-call | flops 1000 | bytes 1000 | tf_op jit(solution)/shard_map/backward/pallas_call | solution.py:61
  73.9 3.9 %backward.7 = f32[3,2688,1536]{2,1,0:T(8,128)} custom-call(bf16[3,24,2688]{2,1,0:T(8,128)(2,1)S(1)} %activate.5.refs_0_.a_ref, bf16[3,24,2688]{2,1,0:T(8,128)(2,1)S(1)} %collective-permute-done.6.b_ref, bf16[3,72,384]{2,1,0:T(8,128)(2,1)S(1)} %activate.9.refs_0_.c_ref, ...), custom_call_target="tpu_custom_call", output_to_operand_aliasing={{}: (5, {})} | custom-call | flops 1000 | bytes 1000 | tf_op jit(solution)/shard_map/backward/pallas_call | solution.py:61
  (34 shorter events, 2.6 us)
Async XLA Ops:
  2.5 13.8 %collective-permute-start.2 = (bf16[2,48,1536]{2,1,0:T(8,128)(2,1)}, bf16[2,48,1536]{2,1,0:T(8,128)(2,1)S(1)}, u32[]{:S(2)}, u32[]{:S(2)}) collective-permute-start(bf16[2,48,1536]{2,1,0:T(8,128)(2,1)} %pick.1.rows_ref.own_ref), channel_id=1, source_target_pairs={{0,4},{4,8},{8,12},{12,0},{1,5},{5,9},{9,13},{13,1},{2,6},{6,10},{... | collective-permute-start | bytes 884744 | tf_op jit(solution)/shard_map/ppermute | solution.py:324
  3.8 13.1 %collective-permute-start.3 = (bf16[2,48,1536]{2,1,0:T(8,128)(2,1)}, bf16[2,48,1536]{2,1,0:T(8,128)(2,1)S(1)}, u32[]{:S(2)}, u32[]{:S(2)}) collective-permute-start(bf16[2,48,1536]{2,1,0:T(8,128)(2,1)} %pick.1.rows_ref.own_ref), channel_id=1, source_target_pairs={{0,12},{4,0},{8,4},{12,8},{1,13},{5,1},{9,5},{13,9},{2,14},{6,2},{... | collective-permute-start | bytes 884744 | tf_op jit(solution)/shard_map/ppermute | solution.py:325
  4.0 1.0 %copy-start = (bf16[2,48,1536]{2,1,0:T(8,128)(2,1)S(1)}, bf16[2,48,1536]{2,1,0:T(8,128)(2,1)}, u32[]{:S(2)}) copy-start(bf16[2,48,1536]{2,1,0:T(8,128)(2,1)} %pick.1.rows_ref.own_ref) | copy-start | bytes 884740
  15.0 7.9 %collective-permute-start = (bf16[3,24,2688]{2,1,0:T(8,128)(2,1)S(1)}, bf16[3,24,2688]{2,1,0:T(8,128)(2,1)S(1)}, u32[]{:S(2)}, u32[]{:S(2)}) collective-permute-start(bf16[3,24,2688]{2,1,0:T(8,128)(2,1)S(1)} %get-tuple-element.28), channel_id=1, source_target_pairs={{0,1},{1,0},{2,3},{3,2},{4,5},{5,4},{6,7},{7,6},{8,9},{9,8},{10,11... | collective-permute-start | bytes 1161224 | tf_op jit(solution)/shard_map/ppermute | solution.py:296
  16.9 9.9 %collective-permute-start.5 = (bf16[2,48,1536]{2,1,0:T(8,128)(2,1)S(1)}, bf16[2,48,1536]{2,1,0:T(8,128)(2,1)S(1)}, u32[]{:S(2)}, u32[]{:S(2)}) collective-permute-start(bf16[2,48,1536]{2,1,0:T(8,128)(2,1)S(1)} %collective-permute-done.3.upper_ref), channel_id=1, source_target_pairs={{8,4},{4,0},{9,5},{5,1},{10,6},{6,2},{11,7},{7,3},{24,20},{20,16},... | collective-permute-start | bytes 884744 | tf_op jit(solution)/shard_map/ppermute | solution.py:329
  20.9 9.7 %collective-permute-start.4 = (bf16[2,48,1536]{2,1,0:T(8,128)(2,1)S(1)}, bf16[2,48,1536]{2,1,0:T(8,128)(2,1)S(1)}, u32[]{:S(2)}, u32[]{:S(2)}) collective-permute-start(bf16[2,48,1536]{2,1,0:T(8,128)(2,1)S(1)} %collective-permute-done.2.lower_ref), channel_id=1, source_target_pairs={{4,8},{8,12},{5,9},{9,13},{6,10},{10,14},{7,11},{11,15},{20,24},{2... | collective-permute-start | bytes 884744 | tf_op jit(solution)/shard_map/ppermute | solution.py:328
  23.0 13.1 %collective-permute-start.1 = (bf16[3,24,2688]{2,1,0:T(8,128)(2,1)S(1)}, bf16[3,24,2688]{2,1,0:T(8,128)(2,1)S(1)}, u32[]{:S(2)}, u32[]{:S(2)}) collective-permute-start(bf16[3,24,2688]{2,1,0:T(8,128)(2,1)S(1)} %get-tuple-element.30), channel_id=1, source_target_pairs={{0,2},{1,3},{2,0},{3,1},{4,6},{5,7},{6,4},{7,5},{8,10},{9,11},{10,... | collective-permute-start | bytes 1161224 | tf_op jit(solution)/shard_map/ppermute | solution.py:300
  30.6 1.0 %copy-start.1 = (bf16[2,48,1536]{2,1,0:T(8,128)(2,1)S(1)}, bf16[2,48,1536]{2,1,0:T(8,128)(2,1)}, u32[]{:S(2)}) copy-start(bf16[2,48,1536]{2,1,0:T(8,128)(2,1)} %pick.1.rows_ref.own_ref) | copy-start | bytes 884740
  34.3 3.0 %collective-permute-start.7 = (bf16[3,72,768]{2,1,0:T(8,128)(2,1)S(1)}, bf16[3,72,768]{2,1,0:T(8,128)(2,1)S(1)}, u32[]{:S(2)}, u32[]{:S(2)}) collective-permute-start(bf16[3,72,768]{2,1,0:T(8,128)(2,1)S(1)} %get-tuple-element.34), channel_id=1, source_target_pairs={{0,1},{1,0},{2,3},{3,2},{4,5},{5,4},{6,7},{7,6},{8,9},{9,8},{10,11... | collective-permute-start | bytes 995336 | tf_op jit(solution)/shard_map/ppermute | solution.py:296
  37.4 11.0 %collective-permute-start.10 = (bf16[3,72,768]{2,1,0:T(8,128)(2,1)S(1)}, bf16[3,72,768]{2,1,0:T(8,128)(2,1)S(1)}, u32[]{:S(2)}, u32[]{:S(2)}) collective-permute-start(bf16[3,72,768]{2,1,0:T(8,128)(2,1)S(1)} %get-tuple-element.42), channel_id=1, source_target_pairs={{0,2},{1,3},{2,0},{3,1},{4,6},{5,7},{6,4},{7,5},{8,10},{9,11},{10,... | collective-permute-start | bytes 995336 | tf_op jit(solution)/shard_map/ppermute | solution.py:300
  41.3 3.4 %collective-permute-start.8 = (bf16[3,72,768]{2,1,0:T(8,128)(2,1)S(1)}, bf16[3,72,768]{2,1,0:T(8,128)(2,1)S(1)}, u32[]{:S(2)}, u32[]{:S(2)}) collective-permute-start(bf16[3,72,768]{2,1,0:T(8,128)(2,1)S(1)} %get-tuple-element.37), channel_id=1, source_target_pairs={{0,1},{1,0},{2,3},{3,2},{4,5},{5,4},{6,7},{7,6},{8,9},{9,8},{10,11... | collective-permute-start | bytes 995336 | tf_op jit(solution)/shard_map/ppermute | solution.py:296
  44.6 2.4 %collective-permute-start.11 = (bf16[3,72,768]{2,1,0:T(8,128)(2,1)S(1)}, bf16[3,72,768]{2,1,0:T(8,128)(2,1)S(1)}, u32[]{:S(2)}, u32[]{:S(2)}) collective-permute-start(bf16[3,72,768]{2,1,0:T(8,128)(2,1)S(1)} %get-tuple-element.43), channel_id=1, source_target_pairs={{0,1},{1,0},{2,3},{3,2},{4,5},{5,4},{6,7},{7,6},{8,9},{9,8},{10,11... | collective-permute-start | bytes 995336 | tf_op jit(solution)/shard_map/ppermute | solution.py:296
  46.1 3.5 %collective-permute-start.9 = (bf16[3,72,384]{2,1,0:T(8,128)(2,1)S(1)}, bf16[3,72,384]{2,1,0:T(8,128)(2,1)S(1)}, u32[]{:S(2)}, u32[]{:S(2)}) collective-permute-start(bf16[3,72,384]{2,1,0:T(8,128)(2,1)S(1)} %get-tuple-element.41), channel_id=1, source_target_pairs={{0,1},{1,0},{2,3},{3,2},{4,5},{5,4},{6,7},{7,6},{8,9},{9,8},{10,11... | collective-permute-start | bytes 497672 | tf_op jit(solution)/shard_map/ppermute | solution.py:296
  46.7 3.3 %collective-permute-start.6 = (bf16[3,24,2688]{2,1,0:T(8,128)(2,1)S(1)}, bf16[3,24,2688]{2,1,0:T(8,128)(2,1)S(1)}, u32[]{:S(2)}, u32[]{:S(2)}) collective-permute-start(bf16[3,24,2688]{2,1,0:T(8,128)(2,1)S(1)} %activate.5.refs_0_.a_ref), channel_id=1, source_target_pairs={{0,1},{1,0},{2,3},{3,2},{4,5},{5,4},{6,7},{7,6},{8,9},{9,8},{10,11... | collective-permute-start | bytes 1161224 | tf_op jit(solution)/shard_map/ppermute | solution.py:296
  46.7 10.2 %collective-permute-start.14 = (bf16[3,72,768]{2,1,0:T(8,128)(2,1)S(1)}, bf16[3,72,768]{2,1,0:T(8,128)(2,1)S(1)}, u32[]{:S(2)}, u32[]{:S(2)}) collective-permute-start(bf16[3,72,768]{2,1,0:T(8,128)(2,1)S(1)} %get-tuple-element.48), channel_id=1, source_target_pairs={{0,2},{1,3},{2,0},{3,1},{4,6},{5,7},{6,4},{7,5},{8,10},{9,11},{10,... | collective-permute-start | bytes 995336 | tf_op jit(solution)/shard_map/ppermute | solution.py:300
  47.1 18.4 %collective-permute-start.13 = (bf16[3,72,768]{2,1,0:T(8,128)(2,1)S(1)}, bf16[3,72,768]{2,1,0:T(8,128)(2,1)S(1)}, u32[]{:S(2)}, u32[]{:S(2)}) collective-permute-start(bf16[3,72,768]{2,1,0:T(8,128)(2,1)S(1)} %get-tuple-element.47), channel_id=1, source_target_pairs={{0,2},{1,3},{2,0},{3,1},{4,6},{5,7},{6,4},{7,5},{8,10},{9,11},{10,... | collective-permute-start | bytes 995336 | tf_op jit(solution)/shard_map/ppermute | solution.py:300
  48.6 2.3 %collective-permute-start.15 = (bf16[3,72,768]{2,1,0:T(8,128)(2,1)S(1)}, bf16[3,72,768]{2,1,0:T(8,128)(2,1)S(1)}, u32[]{:S(2)}, u32[]{:S(2)}) collective-permute-start(bf16[3,72,768]{2,1,0:T(8,128)(2,1)S(1)} %activate.6.refs_0_.c_ref), channel_id=1, source_target_pairs={{0,1},{1,0},{2,3},{3,2},{4,5},{5,4},{6,7},{7,6},{8,9},{9,8},{10,11... | collective-permute-start | bytes 995336 | tf_op jit(solution)/shard_map/ppermute | solution.py:296
  49.7 16.7 %collective-permute-start.12 = (bf16[3,72,384]{2,1,0:T(8,128)(2,1)S(1)}, bf16[3,72,384]{2,1,0:T(8,128)(2,1)S(1)}, u32[]{:S(2)}, u32[]{:S(2)}) collective-permute-start(bf16[3,72,384]{2,1,0:T(8,128)(2,1)S(1)} %get-tuple-element.46), channel_id=1, source_target_pairs={{0,2},{1,3},{2,0},{3,1},{4,6},{5,7},{6,4},{7,5},{8,10},{9,11},{10,... | collective-permute-start | bytes 497672 | tf_op jit(solution)/shard_map/ppermute | solution.py:300
  57.2 2.2 %collective-permute-start.16 = (bf16[3,72,768]{2,1,0:T(8,128)(2,1)S(1)}, bf16[3,72,768]{2,1,0:T(8,128)(2,1)S(1)}, u32[]{:S(2)}, u32[]{:S(2)}) collective-permute-start(bf16[3,72,768]{2,1,0:T(8,128)(2,1)S(1)} %activate.7.refs_0_.c_ref), channel_id=1, source_target_pairs={{0,1},{1,0},{2,3},{3,2},{4,5},{5,4},{6,7},{7,6},{8,9},{9,8},{10,11... | collective-permute-start | bytes 995336 | tf_op jit(solution)/shard_map/ppermute | solution.py:296
  65.6 2.2 %collective-permute-start.18 = (bf16[3,72,768]{2,1,0:T(8,128)(2,1)S(1)}, bf16[3,72,768]{2,1,0:T(8,128)(2,1)S(1)}, u32[]{:S(2)}, u32[]{:S(2)}) collective-permute-start(bf16[3,72,768]{2,1,0:T(8,128)(2,1)S(1)} %activate.8.refs_2_.c_ref), channel_id=1, source_target_pairs={{0,1},{1,0},{2,3},{3,2},{4,5},{5,4},{6,7},{7,6},{8,9},{9,8},{10,11... | collective-permute-start | bytes 995336 | tf_op jit(solution)/shard_map/ppermute | solution.py:296
  66.4 7.5 %collective-permute-start.17 = (bf16[3,72,384]{2,1,0:T(8,128)(2,1)S(1)}, bf16[3,72,384]{2,1,0:T(8,128)(2,1)S(1)}, u32[]{:S(2)}, u32[]{:S(2)}) collective-permute-start(bf16[3,72,384]{2,1,0:T(8,128)(2,1)S(1)} %activate.9.refs_0_.c_ref), channel_id=1, source_target_pairs={{0,1},{1,0},{2,3},{3,2},{4,5},{5,4},{6,7},{7,6},{8,9},{9,8},{10,11... | collective-permute-start | bytes 497672 | tf_op jit(solution)/shard_map/ppermute | solution.py:296
